TPU v7x, 32 devices: a whole 2x2x4 slice. The times are simulated.
32 devices in a mesh: gx: 4 (over z), gy: 2 (over y), gz: 4 (over x, core).
Axes of the slice: x: 2, y: 2, z: 4, core: 2. Of those that a mesh axis runs over, the one named last changes fastest.
Arguments:
- tokens: bfloat16 [1024, 6144], P('gx', ('gy', 'gz')), may hold values from -6 to 6
- weight_in: bfloat16 [6144, 24576], P('gy', ('gx', 'gz')), may hold values from -0.078125 to 0.078125
- weight_out: bfloat16 [24576, 6144], P(('gx', 'gz'), 'gy'), may hold values from -0.0390625 to 0.0390625
- grad_out: bfloat16 [1024, 6144], P('gx', ('gy', 'gz')), may hold values from -6 to 6
Outputs:
- out: bfloat16 [1024, 6144], P('gx', ('gy', 'gz'))
- grad_tokens: bfloat16 [1024, 6144], P('gx', ('gy', 'gz'))
- grad_weight_in: bfloat16 [6144, 24576], P('gy', ('gx', 'gz'))
- grad_weight_out: bfloat16 [24576, 6144], P(('gx', 'gz'), 'gy')
All inputs are finite; a program needn't handle non-finite values.
Results may differ from a plain program's by a relative error of at most 0.025.
Values may be sent and summed in bfloat16 or wider, within the bound.
A program may use at most 192 MiB of HBM per device.

v0:
```python
import jax
import jax.numpy as jnp
from jax import lax
from jax.sharding import PartitionSpec as P

half_root = 0.7071067811865476
inv_root_tau = 0.3989422804014327


def gelu_value(preact):
    return 0.5 * preact * (1.0 + jax.scipy.special.erf(preact * half_root))


def gelu_slope(preact):
    return 0.5 * (
        1.0 + jax.scipy.special.erf(preact * half_root)
    ) + preact * inv_root_tau * jnp.exp(-0.5 * preact * preact)


def contract_rows(left, right):
    return lax.dot_general(
        left, right, (((0,), (0,)), ((), ())), preferred_element_type=jnp.float32
    )


def contract_cols(left, right):
    return lax.dot_general(
        left, right, (((1,), (1,)), ((), ())), preferred_element_type=jnp.float32
    )


def per_device(tokens, weight_in, weight_out, grad_out):
    features = lax.all_gather(tokens, "gz", axis=1, tiled=True)
    grad_feats = lax.all_gather(grad_out, "gz", axis=1, tiled=True)
    full_in = lax.all_gather(weight_in, "gx", axis=1, tiled=True)
    full_out = lax.all_gather(weight_out, "gx", axis=0, tiled=True)
    preact = lax.psum_scatter(
        jnp.dot(features, full_in, preferred_element_type=jnp.float32).astype(jnp.bfloat16),
        "gy",
        scatter_dimension=0,
        tiled=True,
    ).astype(jnp.float32)
    active = gelu_value(preact).astype(jnp.bfloat16)
    active_rows = lax.all_gather(active, "gy", axis=0, tiled=True)
    out_terms = jnp.dot(active_rows, full_out, preferred_element_type=jnp.float32)
    out = lax.psum_scatter(out_terms.astype(jnp.bfloat16), "gz", scatter_dimension=1, tiled=True)
    grad_active = lax.psum_scatter(
        contract_cols(grad_feats, full_out).astype(jnp.bfloat16),
        "gy",
        scatter_dimension=0,
        tiled=True,
    ).astype(jnp.float32)
    grad_preact = (grad_active * gelu_slope(preact)).astype(jnp.bfloat16)
    grad_rows = lax.all_gather(grad_preact, "gy", axis=0, tiled=True)
    grad_weight_out = lax.psum_scatter(
        contract_rows(active_rows, grad_feats).astype(jnp.bfloat16),
        "gx",
        scatter_dimension=0,
        tiled=True,
    )
    grad_weight_in = lax.psum_scatter(
        contract_rows(features, grad_rows).astype(jnp.bfloat16),
        "gx",
        scatter_dimension=1,
        tiled=True,
    )
    token_terms = contract_cols(grad_rows, full_in)
    grad_tokens = lax.psum_scatter(
        token_terms.astype(jnp.bfloat16), "gz", scatter_dimension=1, tiled=True
    )
    return (out, grad_tokens, grad_weight_in, grad_weight_out)


def solution(mesh):
    return jax.shard_map(
        per_device,
        mesh=mesh,
        in_specs=(
            P("gx", ("gy", "gz")),
            P("gy", ("gx", "gz")),
            P(("gx", "gz"), "gy"),
            P("gx", ("gy", "gz")),
        ),
        out_specs=(
            P("gx", ("gy", "gz")),
            P("gx", ("gy", "gz")),
            P("gy", ("gx", "gz")),
            P(("gx", "gz"), "gy"),
        ),
        check_vma=False,
    )
```

profile of v0, /device:TPU:0, one launch (start us, length us, event | category | flops | bytes accessed | tf_op | source)
XLA Modules:
  0.0 2819.3 jit_solution(4847578980471025771)
XLA Ops:
  7.2 0.0 all-gather.15.cloned.1.call-start
  7.2 0.7 all-gather.15.cloned.1.call-update
  7.9 0.0 all-gather.13.cloned.1.call-start
  7.9 0.7 all-gather.13.cloned.1.call-update
  8.6 0.0 all-gather.7.cloned.1.call-start
  8.7 0.7 all-gather.7.cloned.1.call-update
  9.4 0.0 all-gather.9.cloned.1.call-start
  9.4 0.5 all-gather.9.cloned.1.call-update
  10.0 0.0 reduce-scatter.11.cloned.1.call-start
  10.0 21.9 all-gather.15.cloned.1.call-done
  31.9 633.1 %all-gather.13.cloned.1.call-done = bf16[6144,3072]{1,0:T(8,128)(2,1)} async-done(((bf16[1536,3072]{1,0:T(8,128)(2,1)}), bf16[6144,3072]{1,0:T(8,128)(2,1)}) %all-gather.13.cloned.1.call-update) | async-done | bytes 37748752 | tf_op jit(solution)/shard_map/all_gather | solution.py:36
  665.0 18.0 convolution_convert_fusion.1
  683.0 0.0 reduce-scatter.11.cloned.1.call-update
  683.1 0.0 reduce-scatter.7.cloned.1.call-start
  683.1 1.8 all-gather.7.cloned.1.call-done
  684.9 632.9 %all-gather.9.cloned.1.call-done = bf16[3072,6144]{1,0:T(8,128)(2,1)} async-done(((bf16[3072,1536]{1,0:T(8,128)(2,1)}), bf16[3072,6144]{1,0:T(8,128)(2,1)}) %all-gather.9.cloned.1.call-update) | async-done | bytes 37748752 | tf_op jit(solution)/shard_map/all_gather | solution.py:35
  1317.8 20.0 convolution_convert_fusion.2
  1337.7 0.0 reduce-scatter.7.cloned.1.call-update
  1337.8 0.0 all-gather.17.cloned.1.call-start
  1337.8 24.6 reduce-scatter.11.cloned.1.call-done
  1362.4 46.1 %reduce-scatter.7.cloned.1.call-done = bf16[128,6144]{1,0:T(8,128)(2,1)} async-done(((bf16[256,6144]{1,0:T(8,128)(2,1)}), bf16[128,6144]{1,0:T(8,128)(2,1)}) %reduce-scatter.7.cloned.1.call-update) | async-done | bytes 1572880 | tf_op jit(solution)/shard_map/reduce_scatter | solution.py:37
  1408.5 4.3 fusion.7
  1412.8 0.0 copy-start.2
  1412.8 0.0 all-gather.17.cloned.1.call-update
  1412.8 0.0 all-gather.11.cloned.1.call-start
  1412.9 0.7 all-gather.11.cloned.1.call-update
  1413.6 0.0 reduce-scatter.15.cloned.1.call-start
  1413.6 44.3 %all-gather.17.cloned.1.call-done = bf16[256,6144]{1,0:T(8,128)(2,1)} async-done(((bf16[128,6144]{1,0:T(8,128)(2,1)}), bf16[256,6144]{1,0:T(8,128)(2,1)}) %all-gather.17.cloned.1.call-update) | async-done | bytes 3145744 | tf_op jit(solution)/shard_map/all_gather | solution.py:54
  1457.9 0.0 copy-done.2
  1457.9 19.0 convert_bitcast_fusion
  1477.0 0.0 reduce-scatter.15.cloned.1.call-update
  1477.0 0.2 reduce-scatter.13.cloned.1.call-start
  1477.2 1.6 copy-done.1
  1478.8 17.5 convolution_convert_fusion.3
  1496.3 0.0 reduce-scatter.13.cloned.1.call-update
  1496.3 0.0 reduce-scatter.9.cloned.1.call-start
  1496.4 8.6 all-gather.11.cloned.1.call-done
  1505.0 23.5 convolution_convert_fusion.4
  1528.5 0.0 reduce-scatter.9.cloned.1.call-update
  1528.5 0.0 reduce-scatter.17.cloned.1.call-start
  1528.5 0.0 copy-done
  1528.5 17.6 convolution_convert_fusion
  1546.1 0.0 reduce-scatter.17.cloned.1.call-update
  1546.1 580.5 %reduce-scatter.15.cloned.1.call-done = bf16[3072,1536]{0,1:T(8,128)(2,1)} async-done(((bf16[3072,6144]{0,1:T(8,128)(2,1)}), bf16[3072,1536]{0,1:T(8,128)(2,1)}) %reduce-scatter.15.cloned.1.call-update) | async-done | bytes 9437200 | tf_op jit(solution)/shard_map/reduce_scatter | solution.py:61
  2126.6 12.6 copy.8
  2139.2 19.8 reduce-scatter.13.cloned.1.call-done
  2159.0 31.3 %reduce-scatter.9.cloned.1.call-done = bf16[256,768]{1,0:T(8,128)(2,1)} async-done(((bf16[256,3072]{1,0:T(8,128)(2,1)}), bf16[256,768]{1,0:T(8,128)(2,1)}) %reduce-scatter.9.cloned.1.call-update) | async-done | bytes 393232 | tf_op jit(solution)/shard_map/reduce_scatter | solution.py:46
  2190.3 622.2 %reduce-scatter.17.cloned.1.call-done = bf16[1536,3072]{1,0:T(8,128)(2,1)} async-done(((bf16[6144,3072]{1,0:T(8,128)(2,1)}), bf16[1536,3072]{1,0:T(8,128)(2,1)}) %reduce-scatter.17.cloned.1.call-update) | async-done | bytes 9437200 | tf_op jit(solution)/shard_map/reduce_scatter | solution.py:55
  (2 shorter events, 0.0 us)
Async XLA Ops:
  7.2 24.8 all-gather.15.cloned.1.call-start
  7.9 657.1 %all-gather.13.cloned.1.call-start = ((), (), s32[]{:S(2)}) async-start(), calls=%async_computation.10 | async-start | bytes 47185920 | tf_op jit(solution)/shard_map/all_gather | solution.py:36
  8.6 676.2 %all-gather.7.cloned.1.call-start = ((), (), s32[]{:S(2)}) async-start(), calls=%async_computation.6 | async-start | bytes 1966080 | tf_op jit(solution)/shard_map/all_gather | solution.py:33
  9.4 1308.4 %all-gather.9.cloned.1.call-start = ((), (), s32[]{:S(2)}) async-start(), calls=%async_computation.7 | async-start | bytes 47185920 | tf_op jit(solution)/shard_map/all_gather | solution.py:35
  10.0 1352.4 %reduce-scatter.11.cloned.1.call-start = ((), (), s32[]{:S(2)}) async-start(), calls=%async_computation.13 | async-start | bytes 4718592 | tf_op jit(solution)/shard_map/reduce_scatter | solution.py:47
  683.1 725.5 %reduce-scatter.7.cloned.1.call-start = ((), (), s32[]{:S(2)}) async-start(), calls=%async_computation.8 | async-start | bytes 4718592 | tf_op jit(solution)/shard_map/reduce_scatter | solution.py:37
  1337.8 120.1 %all-gather.17.cloned.1.call-start = ((), (), s32[]{:S(2)}) async-start(), calls=%async_computation.14 | async-start | bytes 4718592 | tf_op jit(solution)/shard_map/all_gather | solution.py:54
  1412.8 45.1 %copy-start.2 = (bf16[256,3072]{1,0:T(8,128)(2,1)S(1)}, bf16[256,3072]{1,0:T(8,128)(2,1)}, u32[]{:S(2)}) copy-start(bf16[256,3072]{1,0:T(8,128)(2,1)} %all-gather.7.cloned.1.call-done) | copy-start | bytes 4718596
  1412.8 92.2 %all-gather.11.cloned.1.call-start = ((), (), s32[]{:S(2)}) async-start(), calls=%async_computation.9 | async-start | bytes 4718592 | tf_op jit(solution)/shard_map/all_gather | solution.py:44
  1413.6 713.0 %reduce-scatter.15.cloned.1.call-start = ((), (), s32[]{:S(2)}) async-start(), calls=%async_computation.16 | async-start | bytes 47185920 | tf_op jit(solution)/shard_map/reduce_scatter | solution.py:61
  1477.0 1.9 copy-start.1
  1477.0 682.0 %reduce-scatter.13.cloned.1.call-start = ((), (), s32[]{:S(2)}) async-start(), calls=%async_computation.15 | async-start | bytes 1966080 | tf_op jit(solution)/shard_map/reduce_scatter | solution.py:68
  1496.3 694.0 %reduce-scatter.9.cloned.1.call-start = ((), (), s32[]{:S(2)}) async-start(), calls=%async_computation.11 | async-start | bytes 1966080 | tf_op jit(solution)/shard_map/reduce_scatter | solution.py:46
  1505.0 23.5 copy-start
  1528.5 1284.0 %reduce-scatter.17.cloned.1.call-start = ((), (), s32[]{:S(2)}) async-start(), calls=%async_computation.17 | async-start | bytes 47185920 | tf_op jit(solution)/shard_map/reduce_scatter | solution.py:55
Sparse Core Ops, SparseCore 0:
  9.6 22.3 all-gather.14
  33.5 631.4 all-gather.12
  666.6 18.2 all-gather.6
  686.3 631.4 all-gather.8
  1320.4 41.9 reduce-scatter.10
  1365.2 43.3 reduce-scatter.6
  1412.9 44.9 all-gather.16
  1460.0 44.9 all-gather.10
  1507.4 619.1 reduce-scatter.14
  2129.7 29.2 reduce-scatter.12
  2162.1 28.1 reduce-scatter.8
  2193.2 619.1 reduce-scatter.16
where the time goes:
time: 2820 us
  waiting for transfers between devices  2670 us (95%)
  matrix products  116 us (4%)
    all_gather x1, waiting for transfers between devices, per_device(): full_out = lax.all_gather(weight_out, 'gx', axis=0, tiled=True)  633 us
    all_gather x1, waiting for transfers between devices, per_device(): full_in = lax.all_gather(weight_in, 'gx', axis=1, tiled=True)  633 us
    reduce_scatter x1, waiting for transfers between devices, per_device(): lax.psum_scatter(contract_rows(active_rows, grad_feats).astype(jnp.bfloat...  622 us
    reduce_scatter x1, waiting for transfers between devices, per_device(): lax.psum_scatter(contract_rows(features, grad_rows).astype(jnp.bfloat16),...  580 us
  transfers between devices with their start and end apart: 12, of which 12 were waited for; matrix products, arithmetic and copies ran while one was open for 5% of the time, Pallas kernels for 0%

commit v1 on v0

v1 whole, which is shorter than its diff:
```python
import jax
import jax.numpy as jnp
from jax import lax
from jax.sharding import PartitionSpec as P

half_root = 0.7071067811865476
inv_root_tau = 0.3989422804014327
pieces = 2


def gelu_value(preact):
    return 0.5 * preact * (1.0 + jax.scipy.special.erf(preact * half_root))


def gelu_slope(preact):
    return 0.5 * (
        1.0 + jax.scipy.special.erf(preact * half_root)
    ) + preact * inv_root_tau * jnp.exp(-0.5 * preact * preact)


def contract_rows(left, right):
    return lax.dot_general(
        left, right, (((0,), (0,)), ((), ())), preferred_element_type=jnp.float32
    )


def contract_cols(left, right):
    return lax.dot_general(
        left, right, (((1,), (1,)), ((), ())), preferred_element_type=jnp.float32
    )


def split_rows(values):
    rows = values.shape[0] // pieces
    return [values[at * rows : (at + 1) * rows] for at in range(pieces)]


def gather_tokens(part):
    part = lax.all_gather(part, "gx", axis=0, tiled=True)
    return lax.all_gather(part, "gz", axis=1, tiled=True)


def exchange(partial, width):
    return [
        lax.ppermute(partial, "gy", [(at, (at + shift) % width) for at in range(width)])
        for shift in range(1, width)
    ]


def add_blocks(own, others):
    total = own.astype(jnp.float32)
    for other in others:
        total = total + other.astype(jnp.float32)
    return total


def scatter_terms(terms):
    terms = lax.psum_scatter(
        terms.astype(jnp.bfloat16), "gz", scatter_dimension=1, tiled=True
    )
    return lax.psum_scatter(terms, "gx", scatter_dimension=0, tiled=True)


def solution(mesh):
    width = mesh.shape["gy"]

    def per_device(tokens, weight_in, weight_out, grad_out):
        features = [gather_tokens(part) for part in split_rows(tokens)]
        grad_feats = [gather_tokens(part) for part in split_rows(grad_out)]
        own_pre = [
            jnp.dot(part, weight_in, preferred_element_type=jnp.float32).astype(jnp.bfloat16)
            for part in features
        ]
        far_pre = [exchange(part, width) for part in own_pre]
        own_grad = [
            contract_cols(part, weight_out).astype(jnp.bfloat16) for part in grad_feats
        ]
        far_grad = [exchange(part, width) for part in own_grad]
        preact = [add_blocks(own, far) for own, far in zip(own_pre, far_pre)]
        active = [gelu_value(part).astype(jnp.bfloat16) for part in preact]
        out = [
            scatter_terms(jnp.dot(part, weight_out, preferred_element_type=jnp.float32))
            for part in active
        ]
        grad_preact = [
            (add_blocks(own, far) * gelu_slope(pre)).astype(jnp.bfloat16)
            for own, far, pre in zip(own_grad, far_grad, preact)
        ]
        grad_tokens = [
            scatter_terms(contract_cols(part, weight_in)) for part in grad_preact
        ]
        grad_weight_out = contract_rows(
            jnp.concatenate(active), jnp.concatenate(grad_feats)
        ).astype(jnp.bfloat16)
        grad_weight_in = contract_rows(
            jnp.concatenate(features), jnp.concatenate(grad_preact)
        ).astype(jnp.bfloat16)
        return (
            jnp.concatenate(out),
            jnp.concatenate(grad_tokens),
            grad_weight_in,
            grad_weight_out,
        )

    return jax.shard_map(
        per_device,
        mesh=mesh,
        in_specs=(
            P("gx", ("gy", "gz")),
            P("gy", ("gx", "gz")),
            P(("gx", "gz"), "gy"),
            P("gx", ("gy", "gz")),
        ),
        out_specs=(
            P("gx", ("gy", "gz")),
            P("gx", ("gy", "gz")),
            P("gy", ("gx", "gz")),
            P(("gx", "gz"), "gy"),
        ),
        check_vma=False,
    )
```

time: 2820 us -> 486 us (0.17)
  waiting for transfers between devices: 2670 us -> 265 us
  blocking collectives: 0 us -> 75.6 us
    all_gather x6 -> x4, waiting for transfers between devices: 1340 us -> 0.04 us  [gather_tokens(): return lax.all_gather(part, 'gz', axis=1, tiled=True)]
    reduce_scatter x6 -> x8, waiting for transfers between devices: 1320 us -> 170 us  [the longest x4 86.3 us: scatter_terms(): lax.psum_scatter(terms.astype(jnp.bfloat16), 'gz', scatter_dimension=1, t...]
    ppermute x0 -> x4, waiting for transfers between devices: none -> 94.3 us  [exchange(): lax.ppermute(partial, 'gy', [(at, (at + shift) % width) for at in range(w...]
    all_gather x0 -> x4, blocking collectives: none -> 75.6 us  [gather_tokens(): part = lax.all_gather(part, 'gx', axis=0, tiled=True)]
  transfers between devices with their start and end apart: 12 -> 16, of which waited for: 12 -> 11; matrix products, arithmetic and copies ran while one was open for 5% -> 25% of each run, Pallas kernels for 0% -> 0%
where the time goes in v1:
time: 486 us; the launch traced here: 485 us
  waiting for transfers between devices  265 us (55%)
  matrix products  109 us (22%)
  blocking collectives  75.6 us (16%)
  between operations  14.3 us (3%)
  other arithmetic  11.5 us (2%)
  starting transfers between devices  5.52 us (1%)
    ppermute x4, waiting for transfers between devices, exchange(): lax.ppermute(partial, 'gy', [(at, (at + shift) % width) for at in range(w...  94.3 us
    reduce_scatter x4, waiting for transfers between devices, scatter_terms(): lax.psum_scatter(terms.astype(jnp.bfloat16), 'gz', scatter_dimension=1, t...  86.3 us
    reduce_scatter x4, waiting for transfers between devices, scatter_terms(): return lax.psum_scatter(terms, 'gx', scatter_dimension=0, tiled=True)  83.4 us
    all_gather x4, blocking collectives, gather_tokens(): part = lax.all_gather(part, 'gx', axis=0, tiled=True)  75.6 us
    dot_general x4, matrix products, contract_cols(): lax.dot_general(left, right, (((1,), (1,)), ((), ())), preferred_element_...  40.3 us
    dot_general x2, matrix products, contract_rows(): lax.dot_general(left, right, (((0,), (0,)), ((), ())), preferred_element_...  29.6 us
    dot_general x2, matrix products, per_device(): jnp.dot(part, weight_out, preferred_element_type=jnp.float32)  19.6 us
    dot_general x2, matrix products, per_device(): jnp.dot(part, weight_in, preferred_element_type=jnp.float32)  19.5 us
  transfers between devices with their start and end apart: 16, of which 11 were waited for; matrix products, arithmetic and copies ran while one was open for 25% of the time, Pallas kernels for 0%

profile of v1, /device:TPU:0, one launch (start us, length us, event | category | flops | bytes accessed | tf_op | source)
XLA Modules:
  0.0 485.3 jit_solution(6665577250936390876)
XLA Ops:
  7.2 0.0 all-gather.9.cloned.1.call-start
  7.2 1.0 fusion.24
  8.3 21.7 %all_gather.28 = bf16[512,768]{1,0:T(8,128)(2,1)} all-gather(bf16[128,768]{1,0:T(8,128)(2,1)S(1)} %get-tuple-element.8), channel_id=1, replica_groups=mesh['gx'=4,'gy'=2,'gz'=4] {'gx'}, dimensions={0}, use_global_device_ids=true | all-gather | bytes 983040 | tf_op jit(solution)/shard_map/all_gather | solution.py:39
  30.0 0.0 all-gather.5.cloned.1.call-start
  30.1 1.1 fusion.25
  31.1 18.4 %all_gather.24 = bf16[512,768]{1,0:T(8,128)(2,1)} all-gather(bf16[128,768]{1,0:T(8,128)(2,1)S(1)} %get-tuple-element.10), channel_id=1, replica_groups=mesh['gx'=4,'gy'=2,'gz'=4] {'gx'}, dimensions={0}, use_global_device_ids=true | all-gather | bytes 983040 | tf_op jit(solution)/shard_map/all_gather | solution.py:39
  49.5 0.0 all-gather.11.cloned.1.call-start
  49.5 18.3 %all_gather.30 = bf16[512,768]{1,0:T(8,128)(2,1)} all-gather(bf16[128,768]{1,0:T(8,128)(2,1)S(1)} %get-tuple-element.9), channel_id=1, replica_groups=mesh['gx'=4,'gy'=2,'gz'=4] {'gx'}, dimensions={0}, use_global_device_ids=true | all-gather | bytes 983040 | tf_op jit(solution)/shard_map/all_gather | solution.py:39
  67.9 0.0 all-gather.7.cloned.1.call-start
  67.9 17.2 %all_gather.26 = bf16[512,768]{1,0:T(8,128)(2,1)} all-gather(bf16[128,768]{1,0:T(8,128)(2,1)S(1)} %get-tuple-element.11), channel_id=1, replica_groups=mesh['gx'=4,'gy'=2,'gz'=4] {'gx'}, dimensions={0}, use_global_device_ids=true | all-gather | bytes 983040 | tf_op jit(solution)/shard_map/all_gather | solution.py:39
  85.1 0.0 reduce-scatter.17.cloned.1.call-start
  85.2 9.5 %convolution_convert_fusion.7 = bf16[512,1536]{1,0:T(8,128)(2,1)S(1)} fusion(bf16[512,3072]{1,0:T(8,128)(2,1)} %all-gather.9.cloned.1.call-done, bf16[1536,3072]{1,0:T(8,128)(2,1)} %param.6), kind=kOutput, calls=%fused_computation.37 | convolution fusion | flops 4832624640 | bytes 14155776 | tf_op jit(solution)/shard_map/dot_general | solution.py:28
  94.8 1.6 collective-permute-start.2
  96.3 10.1 %convolution_convert_fusion.9 = bf16[512,1536]{1,0:T(8,128)(2,1)S(1)} fusion(bf16[512,3072]{1,0:T(8,128)(2,1)} %all-gather.5.cloned.1.call-done, bf16[3072,1536]{1,0:T(8,128)(2,1)} %param.5), kind=kOutput, calls=%fused_computation.39 | convolution fusion | flops 4832624640 | bytes 14155776 | tf_op jit(solution)/shard_map/dot_general | solution.py:71
  106.5 0.9 collective-permute-start
  107.4 24.8 %collective-permute-done.2 = bf16[512,1536]{1,0:T(8,128)(2,1)S(1)} collective-permute-done((bf16[512,1536]{1,0:T(8,128)(2,1)S(1)}, bf16[512,1536]{1,0:T(8,128)(2,1)S(1)}, u32[]{:S(2)}, u32[]{:S(2)}) %collective-permute-start.2) | collective-permute-done | bytes 1572896 | tf_op jit(solution)/shard_map/ppermute | solution.py:45
  132.2 1.1 copy-done.2
  133.3 21.6 %collective-permute-done = bf16[512,1536]{1,0:T(8,128)(2,1)S(1)} collective-permute-done((bf16[512,1536]{1,0:T(8,128)(2,1)S(1)}, bf16[512,1536]{1,0:T(8,128)(2,1)S(1)}, u32[]{:S(2)}, u32[]{:S(2)}) %collective-permute-start) | collective-permute-done | bytes 1572896 | tf_op jit(solution)/shard_map/ppermute | solution.py:45
  154.9 3.5 fusion.10
  158.5 10.1 %convolution_convert_fusion.3 = bf16[512,3072]{1,0:T(8,128)(2,1)} fusion(bf16[512,1536]{1,0:T(8,128)(2,1)S(1)} %get-tuple-element.4, bf16[3072,1536]{1,0:T(8,128)(2,1)} %param.5), kind=kOutput, calls=%fused_computation.11 | convolution fusion | flops 4833411072 | bytes 14155776 | tf_op jit(solution)/shard_map/dot_general | solution.py:28
  168.7 0.2 reduce-scatter.21.cloned.1.call-start
  168.9 10.3 %convolution_convert_fusion.6 = bf16[512,1536]{1,0:T(8,128)(2,1)} fusion(bf16[512,3072]{1,0:T(8,128)(2,1)} %all-gather.11.cloned.1.call-done, bf16[1536,3072]{1,0:T(8,128)(2,1)} %param.6), kind=kOutput, calls=%fused_computation.36 | convolution fusion | flops 4832624640 | bytes 14155776 | tf_op jit(solution)/shard_map/dot_general | solution.py:28
  179.2 1.5 collective-permute-start.3
  180.8 9.4 %convolution_convert_fusion.8 = bf16[512,1536]{1,0:T(8,128)(2,1)S(1)} fusion(bf16[512,3072]{1,0:T(8,128)(2,1)} %all-gather.7.cloned.1.call-done, bf16[3072,1536]{1,0:T(8,128)(2,1)} %param.5), kind=kOutput, calls=%fused_computation.38 | convolution fusion | flops 4832624640 | bytes 14155776 | tf_op jit(solution)/shard_map/dot_general | solution.py:71
  190.2 0.7 collective-permute-start.1
  190.8 26.0 %collective-permute-done.3 = bf16[512,1536]{1,0:T(8,128)(2,1)} collective-permute-done((bf16[512,1536]{1,0:T(8,128)(2,1)}, bf16[512,1536]{1,0:T(8,128)(2,1)}, u32[]{:S(2)}, u32[]{:S(2)}) %collective-permute-start.3) | collective-permute-done | bytes 1572896 | tf_op jit(solution)/shard_map/ppermute | solution.py:45
  216.9 21.9 %collective-permute-done.1 = bf16[512,1536]{1,0:T(8,128)(2,1)S(1)} collective-permute-done((bf16[512,1536]{1,0:T(8,128)(2,1)S(1)}, bf16[512,1536]{1,0:T(8,128)(2,1)S(1)}, u32[]{:S(2)}, u32[]{:S(2)}) %collective-permute-start.1) | collective-permute-done | bytes 1572896 | tf_op jit(solution)/shard_map/ppermute | solution.py:45
  238.8 4.4 fusion.15
  243.2 1.2 copy-done
  244.3 10.3 %convolution_convert_fusion.2 = bf16[512,3072]{1,0:T(8,128)(2,1)} fusion(bf16[512,1536]{1,0:T(8,128)(2,1)S(1)} %get-tuple-element.6, bf16[3072,1536]{1,0:T(8,128)(2,1)} %param.5), kind=kOutput, calls=%fused_computation.10 | convolution fusion | flops 4833411072 | bytes 14155776 | tf_op jit(solution)/shard_map/dot_general | solution.py:28
  254.6 0.0 reduce-scatter.9.cloned.1.call-start
  254.7 10.1 %convolution_convert_fusion.5 = bf16[512,3072]{1,0:T(8,128)(2,1)} fusion(bf16[512,1536]{1,0:T(8,128)(2,1)S(1)} %get-tuple-element.5, bf16[1536,3072]{1,0:T(8,128)(2,1)} %param.6), kind=kOutput, calls=%fused_computation.13 | convolution fusion | flops 4833411072 | bytes 14155776 | tf_op jit(solution)/shard_map/dot_general | solution.py:82
  264.8 0.0 reduce-scatter.13.cloned.1.call-start
  264.8 9.5 %convolution_convert_fusion.4 = bf16[512,3072]{1,0:T(8,128)(2,1)} fusion(bf16[512,1536]{1,0:T(8,128)(2,1)} %get-tuple-element.7, bf16[1536,3072]{1,0:T(8,128)(2,1)} %param.6), kind=kOutput, calls=%fused_computation.12 | convolution fusion | flops 4833411072 | bytes 14155776 | tf_op jit(solution)/shard_map/dot_general | solution.py:82
  274.3 0.0 reduce-scatter.19.cloned.1.call-start
  274.4 0.7 reduce-scatter.19.cloned.1.call-update
  275.1 19.1 %reduce-scatter.21.cloned.1.call-done = bf16[512,768]{1,0:T(8,128)(2,1)} async-done(((bf16[512,3072]{1,0:T(8,128)(2,1)}), bf16[512,768]{1,0:T(8,128)(2,1)}) %reduce-scatter.21.cloned.1.call-update) | async-done | bytes 786448 | tf_op jit(solution)/shard_map/reduce_scatter | solution.py:58
  294.3 41.0 %reduce-scatter.9.cloned.1.call-done = bf16[512,768]{1,0:T(8,128)(2,1)} async-done(((bf16[512,3072]{1,0:T(8,128)(2,1)}), bf16[512,768]{1,0:T(8,128)(2,1)}) %reduce-scatter.9.cloned.1.call-update) | async-done | bytes 786448 | tf_op jit(solution)/shard_map/reduce_scatter | solution.py:58
  335.3 0.3 reduce-scatter.15.cloned.1.call-start
  335.6 14.8 %convolution_convert_fusion.1 = bf16[3072,1536]{1,0:T(8,128)(2,1)} fusion(bf16[512,3072]{1,0:T(8,128)(2,1)} %all-gather.7.cloned.1.call-done, bf16[512,3072]{1,0:T(8,128)(2,1)} %all-gather.5.cloned.1.call-done, bf16[512,1536]{1,0:T(8,128)(2,1)} %copy-done, bf16[512,1536]{1,0:T(8,128)(2,1)S(1)} %get-tuple-element.4), kind=kOutput, calls=%fused_computation.1 | convolution fusion | flops 9687269376 | bytes 18874368 | tf_op jit(solution)/shard_map/dot_general | solution.py:22
  350.4 26.2 %reduce-scatter.13.cloned.1.call-done = bf16[512,768]{1,0:T(8,128)(2,1)} async-done(((bf16[512,3072]{1,0:T(8,128)(2,1)}), bf16[512,768]{1,0:T(8,128)(2,1)}) %reduce-scatter.13.cloned.1.call-update) | async-done | bytes 786448 | tf_op jit(solution)/shard_map/reduce_scatter | solution.py:58
  376.6 14.8 %convolution_convert_fusion = bf16[1536,3072]{1,0:T(8,128)(2,1)} fusion(bf16[512,3072]{1,0:T(8,128)(2,1)} %all-gather.11.cloned.1.call-done, bf16[512,3072]{1,0:T(8,128)(2,1)} %all-gather.9.cloned.1.call-done, bf16[512,1536]{1,0:T(8,128)(2,1)} %get-tuple-element.7, bf16[512,1536]{1,0:T(8,128)(2,1)S(1)} %get-tuple-element.5), kind=kOutput, calls=%fused_computation | convolution fusion | flops 9687269376 | bytes 18874368 | tf_op jit(solution)/shard_map/dot_general | solution.py:22
  391.4 10.8 %reduce-scatter.19.cloned.1.call-done = bf16[128,768]{1,0:T(8,128)(2,1)} async-done(((bf16[512,768]{1,0:T(8,128)(2,1)}), bf16[128,768]{1,0:T(8,128)(2,1)}) %reduce-scatter.19.cloned.1.call-update) | async-done | bytes 196624 | tf_op jit(solution)/shard_map/reduce_scatter | solution.py:61
  402.2 24.7 %reduce-scatter.23.cloned.1.call-done = bf16[128,768]{1,0:T(8,128)(2,1)} async-done(((bf16[512,768]{1,0:T(8,128)(2,1)}), bf16[128,768]{1,0:T(8,128)(2,1)}) %reduce-scatter.23.cloned.1.call-update) | async-done | bytes 196624 | tf_op jit(solution)/shard_map/reduce_scatter | solution.py:61
  427.0 1.8 pad_maximum_fusion.1
  428.8 23.1 %reduce-scatter.11.cloned.1.call-done = bf16[128,768]{1,0:T(8,128)(2,1)} async-done(((bf16[512,768]{1,0:T(8,128)(2,1)}), bf16[128,768]{1,0:T(8,128)(2,1)}) %reduce-scatter.11.cloned.1.call-update) | async-done | bytes 196624 | tf_op jit(solution)/shard_map/reduce_scatter | solution.py:61
  451.9 24.8 %reduce-scatter.15.cloned.1.call-done = bf16[128,768]{1,0:T(8,128)(2,1)} async-done(((bf16[512,768]{1,0:T(8,128)(2,1)}), bf16[128,768]{1,0:T(8,128)(2,1)}) %reduce-scatter.15.cloned.1.call-update) | async-done | bytes 196624 | tf_op jit(solution)/shard_map/reduce_scatter | solution.py:61
  476.6 1.8 pad_maximum_fusion
  (22 shorter events, 0.3 us)
Async XLA Ops:
  7.2 78.0 %all-gather.9.cloned.1.call-start = ((), (), s32[]{:S(2)}) async-start(), calls=%async_computation.14 | async-start | bytes 3932160 | tf_op jit(solution)/shard_map/all_gather | solution.py:40
  30.0 66.3 %all-gather.5.cloned.1.call-start = ((), (), s32[]{:S(2)}) async-start(), calls=%async_computation.8 | async-start | bytes 3932160 | tf_op jit(solution)/shard_map/all_gather | solution.py:40
  49.5 119.4 %all-gather.11.cloned.1.call-start = ((), (), s32[]{:S(2)}) async-start(), calls=%async_computation.17 | async-start | bytes 3932160 | tf_op jit(solution)/shard_map/all_gather | solution.py:40
  67.9 112.9 %all-gather.7.cloned.1.call-start = ((), (), s32[]{:S(2)}) async-start(), calls=%async_computation.11 | async-start | bytes 3932160 | tf_op jit(solution)/shard_map/all_gather | solution.py:40
  85.1 189.3 %reduce-scatter.17.cloned.1.call-start = ((), (), s32[]{:S(2)}) async-start(), calls=%async_computation.15 | async-start | bytes 3932160 | tf_op jit(solution)/shard_map/reduce_scatter | solution.py:58
  94.7 11.8 %copy-start.1 = (bf16[512,1536]{1,0:T(8,128)(2,1)}, bf16[512,1536]{1,0:T(8,128)(2,1)S(1)}, u32[]{:S(2)}) copy-start(bf16[512,1536]{1,0:T(8,128)(2,1)S(1)} %convolution_convert_fusion.7) | copy-start | bytes 4718596
  94.8 37.4 %collective-permute-start.2 = (bf16[512,1536]{1,0:T(8,128)(2,1)S(1)}, bf16[512,1536]{1,0:T(8,128)(2,1)S(1)}, u32[]{:S(2)}, u32[]{:S(2)}) collective-permute-start(bf16[512,1536]{1,0:T(8,128)(2,1)S(1)} %convolution_convert_fusion.7), channel_id=1, source_target_pairs={{0,4},{4,0},{1,5},{5,1},{2,6},{6,2},{3,7},{7,3},{8,12},{12,8},{9,1... | collective-permute-start | bytes 4718600 | tf_op jit(solution)/shard_map/ppermute | solution.py:45
  106.5 48.4 %collective-permute-start = (bf16[512,1536]{1,0:T(8,128)(2,1)S(1)}, bf16[512,1536]{1,0:T(8,128)(2,1)S(1)}, u32[]{:S(2)}, u32[]{:S(2)}) collective-permute-start(bf16[512,1536]{1,0:T(8,128)(2,1)S(1)} %convolution_convert_fusion.9), channel_id=1, source_target_pairs={{0,4},{4,0},{1,5},{5,1},{2,6},{6,2},{3,7},{7,3},{8,12},{12,8},{9,1... | collective-permute-start | bytes 4718600 | tf_op jit(solution)/shard_map/ppermute | solution.py:45
  132.2 1.1 copy-start.2
  168.7 125.6 %reduce-scatter.21.cloned.1.call-start = ((), (), s32[]{:S(2)}) async-start(), calls=%async_computation.18 | async-start | bytes 3932160 | tf_op jit(solution)/shard_map/reduce_scatter | solution.py:58
  179.2 37.6 %collective-permute-start.3 = (bf16[512,1536]{1,0:T(8,128)(2,1)}, bf16[512,1536]{1,0:T(8,128)(2,1)}, u32[]{:S(2)}, u32[]{:S(2)}) collective-permute-start(bf16[512,1536]{1,0:T(8,128)(2,1)} %convolution_convert_fusion.6), channel_id=1, source_target_pairs={{0,4},{4,0},{1,5},{5,1},{2,6},{6,2},{3,7},{7,3},{8,12},{12,8},{9,1... | collective-permute-start | bytes 4718600 | tf_op jit(solution)/shard_map/ppermute | solution.py:45
  190.2 48.6 %collective-permute-start.1 = (bf16[512,1536]{1,0:T(8,128)(2,1)S(1)}, bf16[512,1536]{1,0:T(8,128)(2,1)S(1)}, u32[]{:S(2)}, u32[]{:S(2)}) collective-permute-start(bf16[512,1536]{1,0:T(8,128)(2,1)S(1)} %convolution_convert_fusion.8), channel_id=1, source_target_pairs={{0,4},{4,0},{1,5},{5,1},{2,6},{6,2},{3,7},{7,3},{8,12},{12,8},{9,1... | collective-permute-start | bytes 4718600 | tf_op jit(solution)/shard_map/ppermute | solution.py:45
  243.2 1.2 copy-start
  254.6 80.7 %reduce-scatter.9.cloned.1.call-start = ((), (), s32[]{:S(2)}) async-start(), calls=%async_computation.9 | async-start | bytes 3932160 | tf_op jit(solution)/shard_map/reduce_scatter | solution.py:58
  264.8 111.8 %reduce-scatter.13.cloned.1.call-start = ((), (), s32[]{:S(2)}) async-start(), calls=%async_computation.12 | async-start | bytes 3932160 | tf_op jit(solution)/shard_map/reduce_scatter | solution.py:58
  274.3 127.9 %reduce-scatter.19.cloned.1.call-start = ((), (), s32[]{:S(2)}) async-start(), calls=%async_computation.16 | async-start | bytes 983040 | tf_op jit(solution)/shard_map/reduce_scatter | solution.py:61
  275.1 151.9 %reduce-scatter.23.cloned.1.call-start = ((), (), s32[]{:S(2)}) async-start(), calls=%async_computation.19 | async-start | bytes 983040 | tf_op jit(solution)/shard_map/reduce_scatter | solution.py:61
  294.2 157.6 %reduce-scatter.11.cloned.1.call-start = ((), (), s32[]{:S(2)}) async-start(), calls=%async_computation.10 | async-start | bytes 983040 | tf_op jit(solution)/shard_map/reduce_scatter | solution.py:61
  335.3 141.3 %reduce-scatter.15.cloned.1.call-start = ((), (), s32[]{:S(2)}) async-start(), calls=%async_computation.13 | async-start | bytes 983040 | tf_op jit(solution)/shard_map/reduce_scatter | solution.py:61
Sparse Core Ops, SparseCore 0:
  30.1 28.1 all-gather.8
  59.9 28.5 all-gather.4
  90.1 28.5 all-gather.10
  120.1 28.5 all-gather.6
  168.8 38.9 reduce-scatter.16
  254.7 39.4 reduce-scatter.20
  297.3 37.9 reduce-scatter.8
  338.6 37.9 reduce-scatter.12
  378.9 23.3 reduce-scatter.18
  404.4 22.5 reduce-scatter.22
  429.3 22.5 reduce-scatter.10
  454.0 22.5 reduce-scatter.14

commit v2 on v1

--- a/solution.py
+++ b/solution.py
@@ -35,9 +35,21 @@
     return [values[at * rows : (at + 1) * rows] for at in range(pieces)]
 
 
-def gather_tokens(part):
-    part = lax.all_gather(part, "gx", axis=0, tiled=True)
-    return lax.all_gather(part, "gz", axis=1, tiled=True)
+def gather_rows(part, count):
+    rest = [
+        lax.ppermute(part, "gx", [(at, (at + shift) % count) for at in range(count)])
+        for shift in range(1, count)
+    ]
+    return jnp.concatenate([part] + rest)
+
+
+def gather_in_turn(parts, count):
+    gathered = []
+    for part in parts:
+        if gathered:
+            part, gathered[-1] = lax.optimization_barrier((part, gathered[-1]))
+        gathered.append(gather_rows(part, count))
+    return [lax.all_gather(part, "gz", axis=1, tiled=True) for part in gathered]
 
 
 def exchange(partial, width):
@@ -54,19 +66,50 @@
     return total
 
 
-def scatter_terms(terms):
-    terms = lax.psum_scatter(
-        terms.astype(jnp.bfloat16), "gz", scatter_dimension=1, tiled=True
-    )
-    return lax.psum_scatter(terms, "gx", scatter_dimension=0, tiled=True)
+def scatter_near(terms, count):
+    if count != 4:
+        return lax.psum_scatter(terms, "gz", scatter_dimension=1, tiled=True)
+    low = lax.axis_index("gz") % 2
+    block = terms.shape[1] // count
+
+    def columns(at):
+        return lax.dynamic_slice_in_dim(terms, at * block, block, axis=1)
+
+    near = jnp.stack([columns(1 - low), columns(3 - low)])
+    near = lax.ppermute(near, "gz", [(at, at ^ 1) for at in range(count)])
+    own = jnp.stack([columns(low), columns(2 + low)])
+    return (own.astype(jnp.float32) + near.astype(jnp.float32)).astype(jnp.bfloat16)
+
+
+def scatter_far(total, count):
+    if count != 4:
+        return total
+    high = lax.axis_index("gz") // 2
+    far = lax.dynamic_index_in_dim(total, 1 - high, 0, keepdims=False)
+    far = lax.ppermute(far, "gz", [(at, at ^ 2) for at in range(count)])
+    kept = lax.dynamic_index_in_dim(total, high, 0, keepdims=False)
+    return (kept.astype(jnp.float32) + far.astype(jnp.float32)).astype(jnp.bfloat16)
+
+
+def scatter_rows(terms, count):
+    rows = terms.shape[0] // count
+    total = terms[:rows].astype(jnp.float32)
+    for shift in range(1, count):
+        far = lax.ppermute(
+            terms[shift * rows : (shift + 1) * rows],
+            "gx",
+            [(at, (at - shift) % count) for at in range(count)],
+        )
+        total = total + far.astype(jnp.float32)
+    return total.astype(jnp.bfloat16)
 
 
 def solution(mesh):
-    width = mesh.shape["gy"]
+    width, deep, wide = mesh.shape["gy"], mesh.shape["gx"], mesh.shape["gz"]
 
     def per_device(tokens, weight_in, weight_out, grad_out):
-        features = [gather_tokens(part) for part in split_rows(tokens)]
-        grad_feats = [gather_tokens(part) for part in split_rows(grad_out)]
+        gathered = gather_in_turn(split_rows(tokens) + split_rows(grad_out), deep)
+        features, grad_feats = gathered[:pieces], gathered[pieces:]
         own_pre = [
             jnp.dot(part, weight_in, preferred_element_type=jnp.float32).astype(jnp.bfloat16)
             for part in features
@@ -78,20 +121,32 @@
         far_grad = [exchange(part, width) for part in own_grad]
         preact = [add_blocks(own, far) for own, far in zip(own_pre, far_pre)]
         active = [gelu_value(part).astype(jnp.bfloat16) for part in preact]
-        out = [
-            scatter_terms(jnp.dot(part, weight_out, preferred_element_type=jnp.float32))
+        out_near = [
+            scatter_near(
+                jnp.dot(part, weight_out, preferred_element_type=jnp.float32).astype(jnp.bfloat16),
+                wide,
+            )
             for part in active
-        ]
-        grad_preact = [
-            (add_blocks(own, far) * gelu_slope(pre)).astype(jnp.bfloat16)
-            for own, far, pre in zip(own_grad, far_grad, preact)
-        ]
-        grad_tokens = [
-            scatter_terms(contract_cols(part, weight_in)) for part in grad_preact
         ]
         grad_weight_out = contract_rows(
             jnp.concatenate(active), jnp.concatenate(grad_feats)
         ).astype(jnp.bfloat16)
+        out_far, grad_preact, grad_near = [], [], []
+        for at in range(pieces):
+            far, pre_far = far_grad[at], far_pre[at]
+            if at == 0:
+                out_near, far, pre_far = lax.optimization_barrier((out_near, far, pre_far))
+                out_far = [scatter_far(part, wide) for part in out_near]
+            elif at == pieces - 1:
+                unused, out_far, grad_near, far, pre_far = lax.optimization_barrier(
+                    (grad_weight_out[:8, :128], out_far, grad_near, far, pre_far)
+                )
+                out = [scatter_rows(part, deep) for part in out_far]
+            slope = gelu_slope(add_blocks(own_pre[at], pre_far))
+            grad_preact.append((add_blocks(own_grad[at], far) * slope).astype(jnp.bfloat16))
+            terms = contract_cols(grad_preact[at], weight_in).astype(jnp.bfloat16)
+            grad_near.append(scatter_near(terms, wide))
+        grad_tokens = [scatter_rows(scatter_far(part, wide), deep) for part in grad_near]
         grad_weight_in = contract_rows(
             jnp.concatenate(features), jnp.concatenate(grad_preact)
         ).astype(jnp.bfloat16)

time: 486 us -> 347 us (0.71)
  waiting for transfers between devices: 265 us -> 149 us
  blocking collectives: 75.6 us -> 0 us
  starting transfers between devices: 5.52 us -> 44 us
  other arithmetic: 11.5 us -> 25.4 us
  matrix products: 109 us -> 101 us
  local copies, waits for them, and re-layouts: 4.41 us -> 11.8 us
    reduce_scatter x8 -> x0, waiting for transfers between devices: 170 us -> none  [the longest x4 86.3 us: scatter_terms(): lax.psum_scatter(terms.astype(jnp.bfloat16), 'gz', scatter_dimension=1, t...]
    ppermute x0 -> x32, waiting for transfers between devices: none -> 88.1 us  [the longest x12 51.1 us: gather_rows(): lax.ppermute(part, 'gx', [(at, (at + shift) % count) for at in range(coun...]
    all_gather x4 -> x0, blocking collectives: 75.6 us -> none  [gather_tokens(): part = lax.all_gather(part, 'gx', axis=0, tiled=True)]
    ppermute x0 -> x32, starting transfers between devices: none -> 38.6 us  [the longest x12 17.3 us: scatter_rows(): lax.ppermute(terms[shift * rows:(shift + 1) * rows], 'gx', [(at, (at - sh...]
    ppermute x4, waiting for transfers between devices: 94.3 us -> 61 us  [exchange(): lax.ppermute(partial, 'gy', [(at, (at + shift) % width) for at in range(w...]
    convert_element_type x2 -> x16, other arithmetic: 7.95 us -> 16.2 us  [the longest x2 6.34 us: per_device(): (add_blocks(own_grad[at], far) * slope).astype(jnp.bfloat16)]
  transfers between devices with their start and end apart: 16 -> 40, of which waited for: 11 -> 16; matrix products, arithmetic and copies ran while one was open for 25% -> 38% of each run, Pallas kernels for 0% -> 0%
where the time goes in v2:
time: 347 us; the launch traced here: 346 us
  waiting for transfers between devices  149 us (43%)
  matrix products  101 us (29%)
  starting transfers between devices  44 us (13%)
  other arithmetic  25.4 us (7%)
  between operations  14.2 us (4%)
  local copies, waits for them, and re-layouts  11.8 us (3%)
    ppermute x4, waiting for transfers between devices, exchange(): lax.ppermute(partial, 'gy', [(at, (at + shift) % width) for at in range(w...  61 us
    ppermute x12, waiting for transfers between devices, gather_rows(): lax.ppermute(part, 'gx', [(at, (at + shift) % count) for at in range(coun...  51.1 us
    dot_general x4, matrix products, contract_cols(): lax.dot_general(left, right, (((1,), (1,)), ((), ())), preferred_element_...  38.9 us
    dot_general x2, matrix products, contract_rows(): lax.dot_general(left, right, (((0,), (0,)), ((), ())), preferred_element_...  28.3 us
    ppermute x4, waiting for transfers between devices, scatter_far(): far = lax.ppermute(far, 'gz', [(at, at ^ 2) for at in range(count)])  21.5 us
    dot_general x2, matrix products, per_device(): jnp.dot(part, weight_in, preferred_element_type=jnp.float32)  18.8 us
    ppermute x12, starting transfers between devices, scatter_rows(): lax.ppermute(terms[shift * rows:(shift + 1) * rows], 'gx', [(at, (at - sh...  17.3 us
    ppermute x12, starting transfers between devices, gather_rows(): lax.ppermute(part, 'gx', [(at, (at + shift) % count) for at in range(coun...  16.5 us
  transfers between devices with their start and end apart: 40, of which 16 were waited for; matrix products, arithmetic and copies ran while one was open for 38% of the time, Pallas kernels for 0%

profile of v2, /device:TPU:0, one launch (start us, length us, event | category | flops | bytes accessed | tf_op | source)
XLA Modules:
  0.0 345.8 jit_solution(3218860396580595261)
XLA Ops:
  8.3 5.1 %collective-permute-start.2 = (bf16[128,768]{1,0:T(8,128)(2,1)S(1)}, bf16[128,768]{1,0:T(8,128)(2,1)S(1)}, u32[]{:S(2)}, u32[]{:S(2)}) collective-permute-start(bf16[128,768]{1,0:T(8,128)(2,1)S(1)} %get-tuple-element.64), channel_id=1, source_target_pairs={{0,24},{8,0},{16,8},{24,16},{1,25},{9,1},{17,9},{25,17},{2,26},{10... | collective-permute-start | bytes 589832 | tf_op jit(solution)/shard_map/ppermute | solution.py:40
  14.4 4.3 %collective-permute-done.2 = bf16[128,768]{1,0:T(8,128)(2,1)S(1)} collective-permute-done((bf16[128,768]{1,0:T(8,128)(2,1)S(1)}, bf16[128,768]{1,0:T(8,128)(2,1)S(1)}, u32[]{:S(2)}, u32[]{:S(2)}) %collective-permute-start.2) | collective-permute-done | bytes 196640 | tf_op jit(solution)/shard_map/ppermute | solution.py:40
  18.8 11.3 %collective-permute-done.1 = bf16[128,768]{1,0:T(8,128)(2,1)S(1)} collective-permute-done((bf16[128,768]{1,0:T(8,128)(2,1)S(1)}, bf16[128,768]{1,0:T(8,128)(2,1)S(1)}, u32[]{:S(2)}, u32[]{:S(2)}) %collective-permute-start.1) | collective-permute-done | bytes 196640 | tf_op jit(solution)/shard_map/ppermute | solution.py:40
  31.5 2.5 collective-permute-start.6
  34.0 1.9 collective-permute-start.5
  36.0 1.5 collective-permute-done.7
  37.5 13.4 %collective-permute-done.6 = bf16[128,768]{1,0:T(8,128)(2,1)S(1)} collective-permute-done((bf16[128,768]{1,0:T(8,128)(2,1)S(1)}, bf16[128,768]{1,0:T(8,128)(2,1)S(1)}, u32[]{:S(2)}, u32[]{:S(2)}) %collective-permute-start.6) | collective-permute-done | bytes 196640 | tf_op jit(solution)/shard_map/ppermute | solution.py:40
  52.1 1.9 collective-permute-start.10
  54.1 4.3 %collective-permute-done.12 = bf16[128,768]{1,0:T(8,128)(2,1)S(1)} collective-permute-done((bf16[128,768]{1,0:T(8,128)(2,1)S(1)}, bf16[128,768]{1,0:T(8,128)(2,1)S(1)}, u32[]{:S(2)}, u32[]{:S(2)}) %collective-permute-start.12) | collective-permute-done | bytes 196640 | tf_op jit(solution)/shard_map/ppermute | solution.py:40
  58.4 11.5 %collective-permute-done.11 = bf16[128,768]{1,0:T(8,128)(2,1)S(1)} collective-permute-done((bf16[128,768]{1,0:T(8,128)(2,1)S(1)}, bf16[128,768]{1,0:T(8,128)(2,1)S(1)}, u32[]{:S(2)}, u32[]{:S(2)}) %collective-permute-start.11) | collective-permute-done | bytes 196640 | tf_op jit(solution)/shard_map/ppermute | solution.py:40
  71.0 1.4 collective-permute-start.18
  72.4 1.9 collective-permute-start.17
  74.3 9.5 %convolution_convert_fusion.9 = bf16[512,1536]{1,0:T(8,128)(2,1)S(1)} fusion(bf16[512,3072]{1,0:T(8,128)(2,1)} %all-gather.5.cloned.1.call-done, bf16[3072,1536]{1,0:T(8,128)(2,1)} %param.5), kind=kOutput, calls=%fused_computation.43 | convolution fusion | flops 4832624640 | bytes 14155776 | tf_op jit(solution)/shard_map/dot_general | solution.py:114
  83.8 1.6 collective-permute-start.3
  85.4 4.8 %collective-permute-done.18 = bf16[128,768]{1,0:T(8,128)(2,1)} collective-permute-done((bf16[128,768]{1,0:T(8,128)(2,1)S(1)}, bf16[128,768]{1,0:T(8,128)(2,1)}, u32[]{:S(2)}, u32[]{:S(2)}) %collective-permute-start.18) | collective-permute-done | bytes 196640 | tf_op jit(solution)/shard_map/ppermute | solution.py:40
  90.1 2.0 pad_maximum_fusion.7
  92.1 9.4 %convolution_convert_fusion.8 = bf16[512,1536]{1,0:T(8,128)(2,1)S(1)} fusion(bf16[512,3072]{1,0:T(8,128)(2,1)} %all-gather.7.cloned.1.call-done, bf16[3072,1536]{1,0:T(8,128)(2,1)} %param.5), kind=kOutput, calls=%fused_computation.42 | convolution fusion | flops 4832624640 | bytes 14155776 | tf_op jit(solution)/shard_map/dot_general | solution.py:114
  101.5 1.6 collective-permute-start.8
  103.1 18.0 %collective-permute-done.3 = bf16[512,1536]{1,0:T(8,128)(2,1)S(1)} collective-permute-done((bf16[512,1536]{1,0:T(8,128)(2,1)S(1)}, bf16[512,1536]{1,0:T(8,128)(2,1)S(1)}, u32[]{:S(2)}, u32[]{:S(2)}) %collective-permute-start.3) | collective-permute-done | bytes 1572896 | tf_op jit(solution)/shard_map/ppermute | solution.py:57
  122.1 9.9 %convolution_convert_fusion.5 = bf16[512,3072]{1,0:T(8,128)(2,1)S(1)} fusion(bf16[512,1536]{1,0:T(8,128)(2,1)S(1)} %multiply_convert_fusion.1, bf16[1536,3072]{1,0:T(8,128)(2,1)} %param.6), kind=kOutput, calls=%fused_computation.13 | convolution fusion | flops 4833411072 | bytes 14155776 | tf_op jit(solution)/shard_map/dot_general | solution.py:126
  132.0 21.0 %collective-permute-done.8 = bf16[512,1536]{1,0:T(8,128)(2,1)S(1)} collective-permute-done((bf16[512,1536]{1,0:T(8,128)(2,1)S(1)}, bf16[512,1536]{1,0:T(8,128)(2,1)S(1)}, u32[]{:S(2)}, u32[]{:S(2)}) %collective-permute-start.8) | collective-permute-done | bytes 1572896 | tf_op jit(solution)/shard_map/ppermute | solution.py:57
  155.3 5.3 %convolution_convert_fusion.4 = bf16[512,3072]{1,0:T(8,128)(2,1)S(1)} fusion(bf16[512,1536]{1,0:T(8,128)(2,1)S(1)} %multiply_convert_fusion, bf16[1536,3072]{1,0:T(8,128)(2,1)S(1)} %bitcast.69), kind=kOutput, calls=%fused_computation.12 | convolution fusion | flops 4833411072 | bytes 14155776 | tf_op jit(solution)/shard_map/dot_general | solution.py:126
  160.5 2.1 dynamic-slice_bitcast_fusion.15
  165.7 10.3 %convolution_convert_fusion.7 = bf16[512,1536]{1,0:T(8,128)(2,1)} fusion(bf16[512,3072]{1,0:T(8,128)(2,1)} %all-gather.9.cloned.1.call-done, bf16[1536,3072]{1,0:T(8,128)(2,1)} %param.6), kind=kOutput, calls=%fused_computation.41 | convolution fusion | flops 4832624640 | bytes 14155776 | tf_op jit(solution)/shard_map/dot_general | solution.py:28
  176.1 1.5 collective-permute-start.13
  177.6 9.7 %convolution_convert_fusion.6 = bf16[512,1536]{1,0:T(8,128)(2,1)S(1)} fusion(bf16[512,3072]{1,0:T(8,128)(2,1)} %all-gather.11.cloned.1.call-done, bf16[1536,3072]{1,0:T(8,128)(2,1)} %param.6), kind=kOutput, calls=%fused_computation.40 | convolution fusion | flops 4832624640 | bytes 14155776 | tf_op jit(solution)/shard_map/dot_general | solution.py:28
  187.9 1.8 add_convert_fusion.3
  189.8 1.8 add_convert_fusion.2
  191.7 22.0 %collective-permute-done.13 = bf16[512,1536]{1,0:T(8,128)(2,1)} collective-permute-done((bf16[512,1536]{1,0:T(8,128)(2,1)}, bf16[512,1536]{1,0:T(8,128)(2,1)}, u32[]{:S(2)}, u32[]{:S(2)}) %collective-permute-start.13) | collective-permute-done | bytes 1572896 | tf_op jit(solution)/shard_map/ppermute | solution.py:57
  214.6 1.5 collective-permute-start.14
  217.6 3.3 fusion.10
  220.9 9.7 %convolution_convert_fusion.3 = bf16[512,3072]{1,0:T(8,128)(2,1)S(1)} fusion(bf16[512,1536]{1,0:T(8,128)(2,1)S(1)} %fusion.10, bf16[3072,1536]{1,0:T(8,128)(2,1)} %param.5), kind=kOutput, calls=%fused_computation.11 | convolution fusion | flops 4833411072 | bytes 14155776 | tf_op jit(solution)/shard_map/dot_general | solution.py:28
  233.6 14.2 %convolution_convert_fusion = bf16[1536,3072]{1,0:T(8,128)(2,1)} fusion(bf16[512,3072]{1,0:T(8,128)(2,1)} %all-gather.11.cloned.1.call-done, bf16[512,3072]{1,0:T(8,128)(2,1)S(1)} %copy-done.16, bf16[512,1536]{1,0:T(8,128)(2,1)S(1)} %copy-done.11, bf16[512,1536]{1,0:T(8,128)(2,1)S(1)} %copy-done.9), kind=kOutput, calls=%fused_computation | convolution fusion | flops 9687269376 | bytes 18874368 | tf_op jit(solution)/shard_map/dot_general | solution.py:22
  251.6 2.4 collective-permute-start.25
  254.1 1.4 collective-permute-start.24
  256.2 3.0 fusion.15
  259.2 9.1 %convolution_convert_fusion.2 = bf16[512,3072]{1,0:T(8,128)(2,1)S(1)} fusion(bf16[512,1536]{1,0:T(8,128)(2,1)S(1)} %fusion.15, bf16[3072,1536]{1,0:T(8,128)(2,1)} %param.5), kind=kOutput, calls=%fused_computation.10 | convolution fusion | flops 4833411072 | bytes 14155776 | tf_op jit(solution)/shard_map/dot_general | solution.py:28
  270.8 14.2 %convolution_convert_fusion.1 = bf16[3072,1536]{1,0:T(8,128)(2,1)} fusion(bf16[512,3072]{1,0:T(8,128)(2,1)} %all-gather.7.cloned.1.call-done, bf16[512,3072]{1,0:T(8,128)(2,1)S(1)} %copy-done.15, bf16[512,1536]{1,0:T(8,128)(2,1)S(1)} %fusion.15, bf16[512,1536]{1,0:T(8,128)(2,1)S(1)} %copy-done.13), kind=kOutput, calls=%fused_computation.1 | convolution fusion | flops 9687269376 | bytes 18874368 | tf_op jit(solution)/shard_map/dot_general | solution.py:22
  285.1 1.4 collective-permute-start.22
  286.5 2.7 collective-permute-start.21
  289.2 1.5 collective-permute-start.27
  291.9 5.1 %collective-permute-done.22 = bf16[128,768]{1,0:T(8,128)(2,1)S(1)} collective-permute-done((bf16[128,768]{1,0:T(8,128)(2,1)S(1)}, bf16[128,768]{1,0:T(8,128)(2,1)S(1)}, u32[]{:S(2)}, u32[]{:S(2)}) %collective-permute-start.22) | collective-permute-done | bytes 196640 | tf_op jit(solution)/shard_map/ppermute | solution.py:98
  297.9 11.8 %collective-permute-done.27 = bf16[512,768]{1,0:T(8,128)(2,1)S(1)} collective-permute-done((bf16[512,768]{1,0:T(8,128)(2,1)S(1)}, bf16[512,768]{1,0:T(8,128)(2,1)S(1)}, u32[]{:S(2)}, u32[]{:S(2)}) %collective-permute-start.27) | collective-permute-done | bytes 786464 | tf_op jit(solution)/shard_map/ppermute | solution.py:89
  311.2 2.8 collective-permute-start.28
  314.1 9.5 %collective-permute-done.32 = bf16[512,768]{1,0:T(8,128)(2,1)S(1)} collective-permute-done((bf16[512,768]{1,0:T(8,128)(2,1)S(1)}, bf16[512,768]{1,0:T(8,128)(2,1)S(1)}, u32[]{:S(2)}, u32[]{:S(2)}) %collective-permute-start.32) | collective-permute-done | bytes 786464 | tf_op jit(solution)/shard_map/ppermute | solution.py:89
  325.2 2.8 collective-permute-start.33
  328.1 5.5 %collective-permute-done.35 = bf16[128,768]{1,0:T(8,128)(2,1)S(1)} collective-permute-done((bf16[128,768]{1,0:T(8,128)(2,1)S(1)}, bf16[128,768]{1,0:T(8,128)(2,1)S(1)}, u32[]{:S(2)}, u32[]{:S(2)}) %collective-permute-start.35) | collective-permute-done | bytes 196640 | tf_op jit(solution)/shard_map/ppermute | solution.py:98
  333.6 4.8 %collective-permute-done.34 = bf16[128,768]{1,0:T(8,128)(2,1)S(1)} collective-permute-done((bf16[128,768]{1,0:T(8,128)(2,1)S(1)}, bf16[128,768]{1,0:T(8,128)(2,1)S(1)}, u32[]{:S(2)}, u32[]{:S(2)}) %collective-permute-start.34) | collective-permute-done | bytes 196640 | tf_op jit(solution)/shard_map/ppermute | solution.py:98
  (126 shorter events, 31.2 us)
Async XLA Ops:
  7.2 28.8 %copy-start.14 = (bf16[256,768]{1,0:T(8,128)(2,1)S(1)}, bf16[256,768]{1,0:T(8,128)(2,1)}, u32[]{:S(2)}) copy-start(bf16[256,768]{1,0:T(8,128)(2,1)} %param.7) | copy-start | bytes 1179652
  7.2 67.1 %all-gather.5.cloned.1.call-start = ((), (), s32[]{:S(2)}) async-start(), calls=%async_computation | async-start | bytes 3932160 | tf_op jit(solution)/shard_map/all_gather | solution.py:52
  8.3 10.5 %collective-permute-start.2 = (bf16[128,768]{1,0:T(8,128)(2,1)S(1)}, bf16[128,768]{1,0:T(8,128)(2,1)S(1)}, u32[]{:S(2)}, u32[]{:S(2)}) collective-permute-start(bf16[128,768]{1,0:T(8,128)(2,1)S(1)} %get-tuple-element.64), channel_id=1, source_target_pairs={{0,24},{8,0},{16,8},{24,16},{1,25},{9,1},{17,9},{25,17},{2,26},{10... | collective-permute-start | bytes 589832 | tf_op jit(solution)/shard_map/ppermute | solution.py:40
  13.4 16.7 %collective-permute-start.1 = (bf16[128,768]{1,0:T(8,128)(2,1)S(1)}, bf16[128,768]{1,0:T(8,128)(2,1)S(1)}, u32[]{:S(2)}, u32[]{:S(2)}) collective-permute-start(bf16[128,768]{1,0:T(8,128)(2,1)S(1)} %get-tuple-element.64), channel_id=1, source_target_pairs={{0,16},{8,24},{16,0},{24,8},{1,17},{9,25},{17,1},{25,9},{2,18},{10... | collective-permute-start | bytes 589832 | tf_op jit(solution)/shard_map/ppermute | solution.py:40
  13.4 16.7 %collective-permute-start = (bf16[128,768]{1,0:T(8,128)(2,1)S(1)}, bf16[128,768]{1,0:T(8,128)(2,1)S(1)}, u32[]{:S(2)}, u32[]{:S(2)}) collective-permute-start(bf16[128,768]{1,0:T(8,128)(2,1)S(1)} %get-tuple-element.64), channel_id=1, source_target_pairs={{0,8},{8,16},{16,24},{24,0},{1,9},{9,17},{17,25},{25,1},{2,10},{10... | collective-permute-start | bytes 589832 | tf_op jit(solution)/shard_map/ppermute | solution.py:40
  31.1 61.0 %all-gather.7.cloned.1.call-start = ((), (), s32[]{:S(2)}) async-start(), calls=%async_computation.1 | async-start | bytes 3932160 | tf_op jit(solution)/shard_map/all_gather | solution.py:52
  31.1 6.4 %collective-permute-start.7 = (bf16[128,768]{1,0:T(8,128)(2,1)S(1)}, bf16[128,768]{1,0:T(8,128)(2,1)S(1)}, u32[]{:S(2)}, u32[]{:S(2)}) collective-permute-start(bf16[128,768]{1,0:T(8,128)(2,1)S(1)} %get-tuple-element.20), channel_id=1, source_target_pairs={{0,24},{8,0},{16,8},{24,16},{1,25},{9,1},{17,9},{25,17},{2,26},{10... | collective-permute-start | bytes 589832 | tf_op jit(solution)/shard_map/ppermute | solution.py:40
  31.5 19.4 %collective-permute-start.6 = (bf16[128,768]{1,0:T(8,128)(2,1)S(1)}, bf16[128,768]{1,0:T(8,128)(2,1)S(1)}, u32[]{:S(2)}, u32[]{:S(2)}) collective-permute-start(bf16[128,768]{1,0:T(8,128)(2,1)S(1)} %get-tuple-element.20), channel_id=1, source_target_pairs={{0,16},{8,24},{16,0},{24,8},{1,17},{9,25},{17,1},{25,9},{2,18},{10... | collective-permute-start | bytes 589832 | tf_op jit(solution)/shard_map/ppermute | solution.py:40
  34.0 16.9 %collective-permute-start.5 = (bf16[128,768]{1,0:T(8,128)(2,1)S(1)}, bf16[128,768]{1,0:T(8,128)(2,1)S(1)}, u32[]{:S(2)}, u32[]{:S(2)}) collective-permute-start(bf16[128,768]{1,0:T(8,128)(2,1)S(1)} %get-tuple-element.20), channel_id=1, source_target_pairs={{0,8},{8,16},{16,24},{24,0},{1,9},{9,17},{17,25},{25,1},{2,10},{10... | collective-permute-start | bytes 589832 | tf_op jit(solution)/shard_map/ppermute | solution.py:40
  51.9 113.9 %all-gather.9.cloned.1.call-start = ((), (), s32[]{:S(2)}) async-start(), calls=%async_computation.2 | async-start | bytes 3932160 | tf_op jit(solution)/shard_map/all_gather | solution.py:52
  51.9 6.5 %collective-permute-start.12 = (bf16[128,768]{1,0:T(8,128)(2,1)S(1)}, bf16[128,768]{1,0:T(8,128)(2,1)S(1)}, u32[]{:S(2)}, u32[]{:S(2)}) collective-permute-start(bf16[128,768]{1,0:T(8,128)(2,1)S(1)} %get-tuple-element.22), channel_id=1, source_target_pairs={{0,24},{8,0},{16,8},{24,16},{1,25},{9,1},{17,9},{25,17},{2,26},{10... | collective-permute-start | bytes 589832 | tf_op jit(solution)/shard_map/ppermute | solution.py:40
  52.0 17.9 %collective-permute-start.11 = (bf16[128,768]{1,0:T(8,128)(2,1)S(1)}, bf16[128,768]{1,0:T(8,128)(2,1)S(1)}, u32[]{:S(2)}, u32[]{:S(2)}) collective-permute-start(bf16[128,768]{1,0:T(8,128)(2,1)S(1)} %get-tuple-element.22), channel_id=1, source_target_pairs={{0,16},{8,24},{16,0},{24,8},{1,17},{9,25},{17,1},{25,9},{2,18},{10... | collective-permute-start | bytes 589832 | tf_op jit(solution)/shard_map/ppermute | solution.py:40
  52.1 17.8 %collective-permute-start.10 = (bf16[128,768]{1,0:T(8,128)(2,1)S(1)}, bf16[128,768]{1,0:T(8,128)(2,1)S(1)}, u32[]{:S(2)}, u32[]{:S(2)}) collective-permute-start(bf16[128,768]{1,0:T(8,128)(2,1)S(1)} %get-tuple-element.22), channel_id=1, source_target_pairs={{0,8},{8,16},{16,24},{24,0},{1,9},{9,17},{17,25},{25,1},{2,10},{10... | collective-permute-start | bytes 589832 | tf_op jit(solution)/shard_map/ppermute | solution.py:40
  70.8 106.8 %all-gather.11.cloned.1.call-start = ((), (), s32[]{:S(2)}) async-start(), calls=%async_computation.3 | async-start | bytes 3932160 | tf_op jit(solution)/shard_map/all_gather | solution.py:52
  70.9 14.5 %collective-permute-start.19 = (bf16[128,768]{1,0:T(8,128)(2,1)S(1)}, bf16[128,768]{1,0:T(8,128)(2,1)S(1)}, u32[]{:S(2)}, u32[]{:S(2)}) collective-permute-start(bf16[128,768]{1,0:T(8,128)(2,1)S(1)} %get-tuple-element.28), channel_id=1, source_target_pairs={{0,24},{8,0},{16,8},{24,16},{1,25},{9,1},{17,9},{25,17},{2,26},{10... | collective-permute-start | bytes 589832 | tf_op jit(solution)/shard_map/ppermute | solution.py:40
  71.0 19.1 %collective-permute-start.18 = (bf16[128,768]{1,0:T(8,128)(2,1)S(1)}, bf16[128,768]{1,0:T(8,128)(2,1)}, u32[]{:S(2)}, u32[]{:S(2)}) collective-permute-start(bf16[128,768]{1,0:T(8,128)(2,1)S(1)} %get-tuple-element.28), channel_id=1, source_target_pairs={{0,16},{8,24},{16,0},{24,8},{1,17},{9,25},{17,1},{25,9},{2,18},{10... | collective-permute-start | bytes 589832 | tf_op jit(solution)/shard_map/ppermute | solution.py:40
  72.4 17.8 %collective-permute-start.17 = (bf16[128,768]{1,0:T(8,128)(2,1)S(1)}, bf16[128,768]{1,0:T(8,128)(2,1)}, u32[]{:S(2)}, u32[]{:S(2)}) collective-permute-start(bf16[128,768]{1,0:T(8,128)(2,1)S(1)} %get-tuple-element.28), channel_id=1, source_target_pairs={{0,8},{8,16},{16,24},{24,0},{1,9},{9,17},{17,25},{25,1},{2,10},{10... | collective-permute-start | bytes 589832 | tf_op jit(solution)/shard_map/ppermute | solution.py:40
  83.8 37.4 %collective-permute-start.3 = (bf16[512,1536]{1,0:T(8,128)(2,1)S(1)}, bf16[512,1536]{1,0:T(8,128)(2,1)S(1)}, u32[]{:S(2)}, u32[]{:S(2)}) collective-permute-start(bf16[512,1536]{1,0:T(8,128)(2,1)S(1)} %convolution_convert_fusion.9), channel_id=1, source_target_pairs={{0,4},{4,0},{1,5},{5,1},{2,6},{6,2},{3,7},{7,3},{8,12},{12,8},{9,1... | collective-permute-start | bytes 4718600 | tf_op jit(solution)/shard_map/ppermute | solution.py:57
  101.5 51.5 %copy-start = (bf16[512,1536]{1,0:T(8,128)(2,1)}, bf16[512,1536]{1,0:T(8,128)(2,1)S(1)}, u32[]{:S(2)}) copy-start(bf16[512,1536]{1,0:T(8,128)(2,1)S(1)} %convolution_convert_fusion.8) | copy-start | bytes 4718596
  101.5 51.4 %collective-permute-start.8 = (bf16[512,1536]{1,0:T(8,128)(2,1)S(1)}, bf16[512,1536]{1,0:T(8,128)(2,1)S(1)}, u32[]{:S(2)}, u32[]{:S(2)}) collective-permute-start(bf16[512,1536]{1,0:T(8,128)(2,1)S(1)} %convolution_convert_fusion.8), channel_id=1, source_target_pairs={{0,4},{4,0},{1,5},{5,1},{2,6},{6,2},{3,7},{7,3},{8,12},{12,8},{9,1... | collective-permute-start | bytes 4718600 | tf_op jit(solution)/shard_map/ppermute | solution.py:57
  121.2 34.1 %slice-start = ((s8[9437184]{0:T(1024)(128)(4,1)}), s8[4194304]{0:T(1024)(128)(4,1)S(1)}, s32[]{:S(2)}) async-start(s8[9437184]{0:T(1024)(128)(4,1)} %bitcast.68), calls=%async_computation.4 | async-start | bytes 8388608
  122.1 9.9 %copy-start.8 = (bf16[512,1536]{1,0:T(8,128)(2,1)}, bf16[512,1536]{1,0:T(8,128)(2,1)S(1)}, u32[]{:S(2)}) copy-start(bf16[512,1536]{1,0:T(8,128)(2,1)S(1)} %multiply_convert_fusion.1) | copy-start | bytes 4718596
  122.1 33.2 %slice-start.1 = ((s8[9437184]{0:T(1024)(128)(4,1)}), s8[4194304]{0:T(1024)(128)(4,1)S(1)}, s32[]{:S(2)}) async-start(s8[9437184]{0:T(1024)(128)(4,1)} %bitcast.68), calls=%async_computation.5 | async-start | bytes 8388608
  122.1 33.2 %slice-start.2 = ((s8[9437184]{0:T(1024)(128)(4,1)}), s8[1048576]{0:T(1024)(128)(4,1)S(1)}, s32[]{:S(2)}) async-start(s8[9437184]{0:T(1024)(128)(4,1)} %bitcast.68), calls=%async_computation.6 | async-start | bytes 2097152
  164.0 24.0 %collective-permute-start.4 = (bf16[2,512,768]{2,1,0:T(8,128)(2,1)}, bf16[2,512,768]{2,1,0:T(8,128)(2,1)}, u32[]{:S(2)}, u32[]{:S(2)}) collective-permute-start(bf16[2,512,768]{2,1,0:T(8,128)(2,1)} %pad_maximum_fusion), channel_id=1, source_target_pairs={{0,1},{1,0},{2,3},{3,2},{4,5},{5,4},{6,7},{7,6},{8,9},{9,8},{10,11... | collective-permute-start | bytes 4718600 | tf_op jit(solution)/shard_map/ppermute | solution.py:79
  165.2 24.6 %collective-permute-start.9 = (bf16[2,512,768]{2,1,0:T(8,128)(2,1)}, bf16[2,512,768]{2,1,0:T(8,128)(2,1)}, u32[]{:S(2)}, u32[]{:S(2)}) collective-permute-start(bf16[2,512,768]{2,1,0:T(8,128)(2,1)} %pad_maximum_fusion.1), channel_id=1, source_target_pairs={{0,1},{1,0},{2,3},{3,2},{4,5},{5,4},{6,7},{7,6},{8,9},{9,8},{10,11... | collective-permute-start | bytes 4718600 | tf_op jit(solution)/shard_map/ppermute | solution.py:79
  176.1 37.6 %collective-permute-start.13 = (bf16[512,1536]{1,0:T(8,128)(2,1)}, bf16[512,1536]{1,0:T(8,128)(2,1)}, u32[]{:S(2)}, u32[]{:S(2)}) collective-permute-start(bf16[512,1536]{1,0:T(8,128)(2,1)} %convolution_convert_fusion.7), channel_id=1, source_target_pairs={{0,4},{4,0},{1,5},{5,1},{2,6},{6,2},{3,7},{7,3},{8,12},{12,8},{9,1... | collective-permute-start | bytes 4718600 | tf_op jit(solution)/shard_map/ppermute | solution.py:57
  177.6 10.3 %copy-start.6 = (bf16[1,512,768]{2,1,0:T(8,128)(2,1)S(1)}, bf16[1,512,768]{2,1,0:T(8,128)(2,1)}, u32[]{:S(2)}) copy-start(bf16[1,512,768]{2,1,0:T(8,128)(2,1)} %get-tuple-element.66) | copy-start | bytes 2359300
  177.6 10.3 %copy-start.7 = (bf16[1,512,768]{2,1,0:T(8,128)(2,1)S(1)}, bf16[1,512,768]{2,1,0:T(8,128)(2,1)}, u32[]{:S(2)}) copy-start(bf16[1,512,768]{2,1,0:T(8,128)(2,1)} %get-tuple-element.69) | copy-start | bytes 2359300
  187.4 63.9 %collective-permute-start.20 = (bf16[512,1536]{1,0:T(8,128)(2,1)S(1)}, bf16[512,1536]{1,0:T(8,128)(2,1)}, u32[]{:S(2)}, u32[]{:S(2)}) collective-permute-start(bf16[512,1536]{1,0:T(8,128)(2,1)S(1)} %convolution_convert_fusion.6), channel_id=1, source_target_pairs={{0,4},{4,0},{1,5},{5,1},{2,6},{6,2},{3,7},{7,3},{8,12},{12,8},{9,1... | collective-permute-start | bytes 4718600 | tf_op jit(solution)/shard_map/ppermute | solution.py:57
  214.6 33.2 %collective-permute-start.14 = (bf16[512,768]{1,0:T(8,128)(2,1)}, bf16[512,768]{1,0:T(8,128)(2,1)}, u32[]{:S(2)}, u32[]{:S(2)}) collective-permute-start(bf16[512,768]{1,0:T(8,128)(2,1)} %dynamic-slice_bitcast_fusion.11), channel_id=1, source_target_pairs={{0,2},{1,3},{2,0},{3,1},{4,6},{5,7},{6,4},{7,5},{8,10},{9,11},{10,... | collective-permute-start | bytes 2359304 | tf_op jit(solution)/shard_map/ppermute | solution.py:89
  217.1 32.3 %collective-permute-start.15 = (bf16[512,768]{1,0:T(8,128)(2,1)}, bf16[512,768]{1,0:T(8,128)(2,1)}, u32[]{:S(2)}, u32[]{:S(2)}) collective-permute-start(bf16[512,768]{1,0:T(8,128)(2,1)} %dynamic-slice_bitcast_fusion.10), channel_id=1, source_target_pairs={{0,2},{1,3},{2,0},{3,1},{4,6},{5,7},{6,4},{7,5},{8,10},{9,11},{10,... | collective-permute-start | bytes 2359304 | tf_op jit(solution)/shard_map/ppermute | solution.py:89
  231.2 19.6 %collective-permute-start.16 = (bf16[2,512,768]{2,1,0:T(8,128)(2,1)S(1)}, bf16[2,512,768]{2,1,0:T(8,128)(2,1)S(1)}, u32[]{:S(2)}, u32[]{:S(2)}) collective-permute-start(bf16[2,512,768]{2,1,0:T(8,128)(2,1)S(1)} %pad_maximum_fusion.2), channel_id=1, source_target_pairs={{0,1},{1,0},{2,3},{3,2},{4,5},{5,4},{6,7},{7,6},{8,9},{9,8},{10,11... | collective-permute-start | bytes 4718600 | tf_op jit(solution)/shard_map/ppermute | solution.py:79
  251.3 33.8 %collective-permute-start.26 = (bf16[128,768]{1,0:T(8,128)(2,1)S(1)}, bf16[128,768]{1,0:T(8,128)(2,1)S(1)}, u32[]{:S(2)}, u32[]{:S(2)}) collective-permute-start(bf16[128,768]{1,0:T(8,128)(2,1)S(1)} %get-tuple-element.60), channel_id=1, source_target_pairs={{0,8},{8,16},{16,24},{24,0},{1,9},{9,17},{17,25},{25,1},{2,10},{10... | collective-permute-start | bytes 589832 | tf_op jit(solution)/shard_map/ppermute | solution.py:98
  251.6 34.9 %collective-permute-start.25 = (bf16[128,768]{1,0:T(8,128)(2,1)S(1)}, bf16[128,768]{1,0:T(8,128)(2,1)S(1)}, u32[]{:S(2)}, u32[]{:S(2)}) collective-permute-start(bf16[128,768]{1,0:T(8,128)(2,1)S(1)} %get-tuple-element.61), channel_id=1, source_target_pairs={{0,16},{8,24},{16,0},{24,8},{1,17},{9,25},{17,1},{25,9},{2,18},{10... | collective-permute-start | bytes 589832 | tf_op jit(solution)/shard_map/ppermute | solution.py:98
  254.1 35.1 %collective-permute-start.24 = (bf16[128,768]{1,0:T(8,128)(2,1)S(1)}, bf16[128,768]{1,0:T(8,128)(2,1)S(1)}, u32[]{:S(2)}, u32[]{:S(2)}) collective-permute-start(bf16[128,768]{1,0:T(8,128)(2,1)S(1)} %get-tuple-element.59), channel_id=1, source_target_pairs={{0,24},{8,0},{16,8},{24,16},{1,25},{9,1},{17,9},{25,17},{2,26},{10... | collective-permute-start | bytes 589832 | tf_op jit(solution)/shard_map/ppermute | solution.py:98
  255.5 36.4 %collective-permute-start.23 = (bf16[128,768]{1,0:T(8,128)(2,1)S(1)}, bf16[128,768]{1,0:T(8,128)(2,1)S(1)}, u32[]{:S(2)}, u32[]{:S(2)}) collective-permute-start(bf16[128,768]{1,0:T(8,128)(2,1)S(1)} %get-tuple-element.57), channel_id=1, source_target_pairs={{0,8},{8,16},{16,24},{24,0},{1,9},{9,17},{17,25},{25,1},{2,10},{10... | collective-permute-start | bytes 589832 | tf_op jit(solution)/shard_map/ppermute | solution.py:98
  268.9 21.9 %collective-permute-start.31 = (bf16[2,512,768]{2,1,0:T(8,128)(2,1)S(1)}, bf16[2,512,768]{2,1,0:T(8,128)(2,1)S(1)}, u32[]{:S(2)}, u32[]{:S(2)}) collective-permute-start(bf16[2,512,768]{2,1,0:T(8,128)(2,1)S(1)} %pad_maximum_fusion.3), channel_id=1, source_target_pairs={{0,1},{1,0},{2,3},{3,2},{4,5},{5,4},{6,7},{7,6},{8,9},{9,8},{10,11... | collective-permute-start | bytes 4718600 | tf_op jit(solution)/shard_map/ppermute | solution.py:79
  285.1 11.9 %collective-permute-start.22 = (bf16[128,768]{1,0:T(8,128)(2,1)S(1)}, bf16[128,768]{1,0:T(8,128)(2,1)S(1)}, u32[]{:S(2)}, u32[]{:S(2)}) collective-permute-start(bf16[128,768]{1,0:T(8,128)(2,1)S(1)} %get-tuple-element.58), channel_id=1, source_target_pairs={{0,16},{8,24},{16,0},{24,8},{1,17},{9,25},{17,1},{25,9},{2,18},{10... | collective-permute-start | bytes 589832 | tf_op jit(solution)/shard_map/ppermute | solution.py:98
  286.5 10.5 %collective-permute-start.21 = (bf16[128,768]{1,0:T(8,128)(2,1)S(1)}, bf16[128,768]{1,0:T(8,128)(2,1)S(1)}, u32[]{:S(2)}, u32[]{:S(2)}) collective-permute-start(bf16[128,768]{1,0:T(8,128)(2,1)S(1)} %get-tuple-element.56), channel_id=1, source_target_pairs={{0,24},{8,0},{16,8},{24,16},{1,25},{9,1},{17,9},{25,17},{2,26},{10... | collective-permute-start | bytes 589832 | tf_op jit(solution)/shard_map/ppermute | solution.py:98
  289.2 20.5 %collective-permute-start.27 = (bf16[512,768]{1,0:T(8,128)(2,1)S(1)}, bf16[512,768]{1,0:T(8,128)(2,1)S(1)}, u32[]{:S(2)}, u32[]{:S(2)}) collective-permute-start(bf16[512,768]{1,0:T(8,128)(2,1)S(1)} %dynamic-slice_bitcast_fusion.5), channel_id=1, source_target_pairs={{0,2},{1,3},{2,0},{3,1},{4,6},{5,7},{6,4},{7,5},{8,10},{9,11},{10,... | collective-permute-start | bytes 2359304 | tf_op jit(solution)/shard_map/ppermute | solution.py:89
  291.3 32.3 %collective-permute-start.32 = (bf16[512,768]{1,0:T(8,128)(2,1)S(1)}, bf16[512,768]{1,0:T(8,128)(2,1)S(1)}, u32[]{:S(2)}, u32[]{:S(2)}) collective-permute-start(bf16[512,768]{1,0:T(8,128)(2,1)S(1)} %dynamic-slice_bitcast_fusion), channel_id=1, source_target_pairs={{0,2},{1,3},{2,0},{3,1},{4,6},{5,7},{6,4},{7,5},{8,10},{9,11},{10,... | collective-permute-start | bytes 2359304 | tf_op jit(solution)/shard_map/ppermute | solution.py:89
  309.9 15.3 %collective-permute-start.30 = (bf16[128,768]{1,0:T(8,128)(2,1)S(1)}, bf16[128,768]{1,0:T(8,128)(2,1)S(1)}, u32[]{:S(2)}, u32[]{:S(2)}) collective-permute-start(bf16[128,768]{1,0:T(8,128)(2,1)S(1)} %get-tuple-element.51), channel_id=1, source_target_pairs={{0,8},{8,16},{16,24},{24,0},{1,9},{9,17},{17,25},{25,1},{2,10},{10... | collective-permute-start | bytes 589832 | tf_op jit(solution)/shard_map/ppermute | solution.py:98
  310.0 18.1 %collective-permute-start.29 = (bf16[128,768]{1,0:T(8,128)(2,1)S(1)}, bf16[128,768]{1,0:T(8,128)(2,1)S(1)}, u32[]{:S(2)}, u32[]{:S(2)}) collective-permute-start(bf16[128,768]{1,0:T(8,128)(2,1)S(1)} %get-tuple-element.52), channel_id=1, source_target_pairs={{0,16},{8,24},{16,0},{24,8},{1,17},{9,25},{17,1},{25,9},{2,18},{10... | collective-permute-start | bytes 589832 | tf_op jit(solution)/shard_map/ppermute | solution.py:98
  311.2 16.8 %collective-permute-start.28 = (bf16[128,768]{1,0:T(8,128)(2,1)S(1)}, bf16[128,768]{1,0:T(8,128)(2,1)S(1)}, u32[]{:S(2)}, u32[]{:S(2)}) collective-permute-start(bf16[128,768]{1,0:T(8,128)(2,1)S(1)} %get-tuple-element.50), channel_id=1, source_target_pairs={{0,24},{8,0},{16,8},{24,16},{1,25},{9,1},{17,9},{25,17},{2,26},{10... | collective-permute-start | bytes 589832 | tf_op jit(solution)/shard_map/ppermute | solution.py:98
  323.9 9.7 %collective-permute-start.35 = (bf16[128,768]{1,0:T(8,128)(2,1)S(1)}, bf16[128,768]{1,0:T(8,128)(2,1)S(1)}, u32[]{:S(2)}, u32[]{:S(2)}) collective-permute-start(bf16[128,768]{1,0:T(8,128)(2,1)S(1)} %get-tuple-element.54), channel_id=1, source_target_pairs={{0,8},{8,16},{16,24},{24,0},{1,9},{9,17},{17,25},{25,1},{2,10},{10... | collective-permute-start | bytes 589832 | tf_op jit(solution)/shard_map/ppermute | solution.py:98
  324.0 14.4 %collective-permute-start.34 = (bf16[128,768]{1,0:T(8,128)(2,1)S(1)}, bf16[128,768]{1,0:T(8,128)(2,1)S(1)}, u32[]{:S(2)}, u32[]{:S(2)}) collective-permute-start(bf16[128,768]{1,0:T(8,128)(2,1)S(1)} %get-tuple-element.55), channel_id=1, source_target_pairs={{0,16},{8,24},{16,0},{24,8},{1,17},{9,25},{17,1},{25,9},{2,18},{10... | collective-permute-start | bytes 589832 | tf_op jit(solution)/shard_map/ppermute | solution.py:98
  325.2 13.2 %collective-permute-start.33 = (bf16[128,768]{1,0:T(8,128)(2,1)S(1)}, bf16[128,768]{1,0:T(8,128)(2,1)S(1)}, u32[]{:S(2)}, u32[]{:S(2)}) collective-permute-start(bf16[128,768]{1,0:T(8,128)(2,1)S(1)} %get-tuple-element.53), channel_id=1, source_target_pairs={{0,24},{8,0},{16,8},{24,16},{1,25},{9,1},{17,9},{25,17},{2,26},{10... | collective-permute-start | bytes 589832 | tf_op jit(solution)/shard_map/ppermute | solution.py:98
  (12 other events, 38.2 us)
Sparse Core Ops, SparseCore 0:
  31.2 28.9 all-gather.4
  62.3 28.5 all-gather.6
  92.5 28.5 all-gather.8
  122.5 28.5 all-gather.10

commit v3 on v2

--- a/solution.py
+++ b/solution.py
@@ -43,13 +43,8 @@
     return jnp.concatenate([part] + rest)
 
 
-def gather_in_turn(parts, count):
-    gathered = []
-    for part in parts:
-        if gathered:
-            part, gathered[-1] = lax.optimization_barrier((part, gathered[-1]))
-        gathered.append(gather_rows(part, count))
-    return [lax.all_gather(part, "gz", axis=1, tiled=True) for part in gathered]
+def after(value, *earlier):
+    return lax.optimization_barrier((value,) + earlier)[0]
 
 
 def exchange(partial, width):
@@ -108,17 +103,29 @@
     width, deep, wide = mesh.shape["gy"], mesh.shape["gx"], mesh.shape["gz"]
 
     def per_device(tokens, weight_in, weight_out, grad_out):
-        gathered = gather_in_turn(split_rows(tokens) + split_rows(grad_out), deep)
+        def project(part):
+            product = jnp.dot(part, weight_in, preferred_element_type=jnp.float32)
+            return product.astype(jnp.bfloat16)
+
+        parts = split_rows(tokens) + split_rows(grad_out)
+        rows, gathered, own_pre = None, [], []
+        for at, part in enumerate(parts):
+            if at:
+                part, rows = lax.optimization_barrier((part, rows))
+                gathered.append(lax.all_gather(rows, "gz", axis=1, tiled=True))
+            if at >= pieces:
+                own_pre.append(project(gathered[at - pieces]))
+                part = after(part, own_pre[-1])
+            rows = gather_rows(part, deep)
+        gathered.append(lax.all_gather(rows, "gz", axis=1, tiled=True))
         features, grad_feats = gathered[:pieces], gathered[pieces:]
-        own_pre = [
-            jnp.dot(part, weight_in, preferred_element_type=jnp.float32).astype(jnp.bfloat16)
-            for part in features
-        ]
         far_pre = [exchange(part, width) for part in own_pre]
-        own_grad = [
-            contract_cols(part, weight_out).astype(jnp.bfloat16) for part in grad_feats
-        ]
-        far_grad = [exchange(part, width) for part in own_grad]
+        own_grad = jnp.concatenate(
+            [contract_cols(part, weight_out).astype(jnp.bfloat16) for part in grad_feats]
+        )
+        own_grad, far_pre[1:] = lax.optimization_barrier((own_grad, far_pre[1:]))
+        far_grad = exchange(own_grad, width)
+        own_grad = split_rows(own_grad)
         preact = [add_blocks(own, far) for own, far in zip(own_pre, far_pre)]
         active = [gelu_value(part).astype(jnp.bfloat16) for part in preact]
         out_near = [
@@ -128,27 +135,28 @@
             )
             for part in active
         ]
-        grad_weight_out = contract_rows(
-            jnp.concatenate(active), jnp.concatenate(grad_feats)
-        ).astype(jnp.bfloat16)
-        out_far, grad_preact, grad_near = [], [], []
+        out_far = [scatter_far(part, wide) for part in out_near]
+        out_far, far_grad, far_pre = lax.optimization_barrier((out_far, far_grad, far_pre))
+        far_grad = list(zip(*[split_rows(part) for part in far_grad]))
+        grad_preact, grad_near = [], []
         for at in range(pieces):
             far, pre_far = far_grad[at], far_pre[at]
-            if at == 0:
-                out_near, far, pre_far = lax.optimization_barrier((out_near, far, pre_far))
-                out_far = [scatter_far(part, wide) for part in out_near]
-            elif at == pieces - 1:
-                unused, out_far, grad_near, far, pre_far = lax.optimization_barrier(
-                    (grad_weight_out[:8, :128], out_far, grad_near, far, pre_far)
-                )
-                out = [scatter_rows(part, deep) for part in out_far]
             slope = gelu_slope(add_blocks(own_pre[at], pre_far))
             grad_preact.append((add_blocks(own_grad[at], far) * slope).astype(jnp.bfloat16))
             terms = contract_cols(grad_preact[at], weight_in).astype(jnp.bfloat16)
             grad_near.append(scatter_near(terms, wide))
-        grad_tokens = [scatter_rows(scatter_far(part, wide), deep) for part in grad_near]
+        out = [scatter_rows(part, deep) for part in out_far]
+        grad_far = [scatter_far(part, wide) for part in grad_near[:-1]]
+        grad_near[-1], grad_far, last, last_active = lax.optimization_barrier(
+            (grad_near[-1], grad_far, grad_preact[-1], active[-1])
+        )
+        grad_far.append(scatter_far(grad_near[-1], wide))
+        grad_tokens = [scatter_rows(part, deep) for part in grad_far]
         grad_weight_in = contract_rows(
-            jnp.concatenate(features), jnp.concatenate(grad_preact)
+            jnp.concatenate(features), jnp.concatenate(grad_preact[:-1] + [last])
+        ).astype(jnp.bfloat16)
+        grad_weight_out = contract_rows(
+            jnp.concatenate(active[:-1] + [last_active]), jnp.concatenate(grad_feats)
         ).astype(jnp.bfloat16)
         return (
             jnp.concatenate(out),

time: 347 us -> 387 us (1.12)
  waiting for transfers between devices: 149 us -> 180 us
  starting transfers between devices: 44 us -> 56.9 us
  local copies, waits for them, and re-layouts: 11.8 us -> 7.74 us
    ppermute x12, waiting for transfers between devices: 15.4 us -> 34.7 us  [scatter_rows(): lax.ppermute(terms[shift * rows:(shift + 1) * rows], 'gx', [(at, (at - sh...]
    ppermute x4 -> x3, waiting for transfers between devices: 61 us -> 43.4 us  [exchange(): lax.ppermute(partial, 'gy', [(at, (at + shift) % width) for at in range(w...]
    ppermute x4, waiting for transfers between devices: 21.5 us -> 33.2 us  [scatter_far(): far = lax.ppermute(far, 'gz', [(at, at ^ 2) for at in range(count)])]
    ppermute x12, starting transfers between devices: 17.3 us -> 27.9 us  [scatter_rows(): lax.ppermute(terms[shift * rows:(shift + 1) * rows], 'gx', [(at, (at - sh...]
    ppermute x12, waiting for transfers between devices: 51.1 us -> 60.7 us  [gather_rows(): lax.ppermute(part, 'gx', [(at, (at + shift) % count) for at in range(coun...]
    all_gather x4, waiting for transfers between devices: 0.03 us -> 8.31 us  [per_device(): gathered.append(lax.all_gather(rows, 'gz', axis=1, tiled=True))]
    unnamed x40 -> x38, local copies, waits for them, and re-layouts: 5.55 us -> 0.38 us
    dot_general x4, matrix products: 38.9 us -> 34.4 us  [contract_cols(): lax.dot_general(left, right, (((1,), (1,)), ((), ())), preferred_element_...]
  transfers between devices with their start and end apart: 40 -> 39, of which waited for: 16 -> 20; matrix products, arithmetic and copies ran while one was open for 38% -> 29% of each run, Pallas kernels for 0% -> 0%
where the time goes in v3:
time: 387 us; the launch traced here: 386 us
  waiting for transfers between devices  180 us (47%)
  matrix products  101 us (26%)
  starting transfers between devices  56.9 us (15%)
  other arithmetic  26.3 us (7%)
  between operations  14.2 us (4%)
  local copies, waits for them, and re-layouts  7.74 us (2%)
    ppermute x12, waiting for transfers between devices, gather_rows(): lax.ppermute(part, 'gx', [(at, (at + shift) % count) for at in range(coun...  60.7 us
    ppermute x3, waiting for transfers between devices, exchange(): lax.ppermute(partial, 'gy', [(at, (at + shift) % width) for at in range(w...  43.4 us
    ppermute x12, waiting for transfers between devices, scatter_rows(): lax.ppermute(terms[shift * rows:(shift + 1) * rows], 'gx', [(at, (at - sh...  34.7 us
    dot_general x4, matrix products, contract_cols(): lax.dot_general(left, right, (((1,), (1,)), ((), ())), preferred_element_...  34.4 us
    ppermute x4, waiting for transfers between devices, scatter_far(): far = lax.ppermute(far, 'gz', [(at, at ^ 2) for at in range(count)])  33.2 us
    ppermute x12, starting transfers between devices, scatter_rows(): lax.ppermute(terms[shift * rows:(shift + 1) * rows], 'gx', [(at, (at - sh...  27.9 us
    dot_general x2, matrix products, contract_rows(): lax.dot_general(left, right, (((0,), (0,)), ((), ())), preferred_element_...  27.5 us
    ppermute x12, starting transfers between devices, gather_rows(): lax.ppermute(part, 'gx', [(at, (at + shift) % count) for at in range(coun...  20.2 us
  transfers between devices with their start and end apart: 39, of which 20 were waited for; matrix products, arithmetic and copies ran while one was open for 29% of the time, Pallas kernels for 0%

profile of v3, /device:TPU:0, one launch (start us, length us, event | category | flops | bytes accessed | tf_op | source)
XLA Modules:
  0.0 386.4 jit_solution(8075227249143224856)
XLA Ops:
  8.3 5.1 %collective-permute-start.2 = (bf16[128,768]{1,0:T(8,128)(2,1)S(1)}, bf16[128,768]{1,0:T(8,128)(2,1)S(1)}, u32[]{:S(2)}, u32[]{:S(2)}) collective-permute-start(bf16[128,768]{1,0:T(8,128)(2,1)S(1)} %get-tuple-element.74), channel_id=1, source_target_pairs={{0,24},{8,0},{16,8},{24,16},{1,25},{9,1},{17,9},{25,17},{2,26},{10... | collective-permute-start | bytes 589832 | tf_op jit(solution)/shard_map/ppermute | solution.py:40
  14.4 4.3 %collective-permute-done.2 = bf16[128,768]{1,0:T(8,128)(2,1)S(1)} collective-permute-done((bf16[128,768]{1,0:T(8,128)(2,1)S(1)}, bf16[128,768]{1,0:T(8,128)(2,1)S(1)}, u32[]{:S(2)}, u32[]{:S(2)}) %collective-permute-start.2) | collective-permute-done | bytes 196640 | tf_op jit(solution)/shard_map/ppermute | solution.py:40
  18.8 11.3 %collective-permute-done.1 = bf16[128,768]{1,0:T(8,128)(2,1)S(1)} collective-permute-done((bf16[128,768]{1,0:T(8,128)(2,1)S(1)}, bf16[128,768]{1,0:T(8,128)(2,1)S(1)}, u32[]{:S(2)}, u32[]{:S(2)}) %collective-permute-start.1) | collective-permute-done | bytes 196640 | tf_op jit(solution)/shard_map/ppermute | solution.py:40
  31.5 2.5 collective-permute-start.7
  34.0 1.9 collective-permute-start.6
  37.5 13.4 %collective-permute-done.7 = bf16[128,768]{1,0:T(8,128)(2,1)S(1)} collective-permute-done((bf16[128,768]{1,0:T(8,128)(2,1)S(1)}, bf16[128,768]{1,0:T(8,128)(2,1)S(1)}, u32[]{:S(2)}, u32[]{:S(2)}) %collective-permute-start.7) | collective-permute-done | bytes 196640 | tf_op jit(solution)/shard_map/ppermute | solution.py:40
  51.9 8.3 %all-gather.5.cloned.1.call-done = bf16[512,3072]{1,0:T(8,128)(2,1)} async-done(((bf16[512,768]{1,0:T(8,128)(2,1)}), bf16[512,3072]{1,0:T(8,128)(2,1)}) %all-gather.5.cloned.1.call-update) | async-done | bytes 3145744 | tf_op jit(solution)/shard_map/all_gather | solution.py:115
  60.2 9.4 %convolution_convert_fusion.9 = bf16[512,1536]{1,0:T(8,128)(2,1)S(1)} fusion(bf16[512,3072]{1,0:T(8,128)(2,1)} %all-gather.5.cloned.1.call-done, bf16[3072,1536]{1,0:T(8,128)(2,1)} %param.5), kind=kOutput, calls=%fused_computation.44 | convolution fusion | flops 4832624640 | bytes 14155776 | tf_op jit(solution)/shard_map/dot_general | solution.py:107
  69.6 3.4 collective-permute-start.11
  74.1 4.2 %collective-permute-done.11 = bf16[128,768]{1,0:T(8,128)(2,1)S(1)} collective-permute-done((bf16[128,768]{1,0:T(8,128)(2,1)S(1)}, bf16[128,768]{1,0:T(8,128)(2,1)S(1)}, u32[]{:S(2)}, u32[]{:S(2)}) %collective-permute-start.11) | collective-permute-done | bytes 196640 | tf_op jit(solution)/shard_map/ppermute | solution.py:40
  78.3 11.9 %collective-permute-done.10 = bf16[128,768]{1,0:T(8,128)(2,1)S(1)} collective-permute-done((bf16[128,768]{1,0:T(8,128)(2,1)S(1)}, bf16[128,768]{1,0:T(8,128)(2,1)S(1)}, u32[]{:S(2)}, u32[]{:S(2)}) %collective-permute-start.10) | collective-permute-done | bytes 196640 | tf_op jit(solution)/shard_map/ppermute | solution.py:40
  91.3 10.3 %convolution_convert_fusion.8 = bf16[512,1536]{1,0:T(8,128)(2,1)} fusion(bf16[512,3072]{1,0:T(8,128)(2,1)} %all-gather.7.cloned.1.call-done, bf16[3072,1536]{1,0:T(8,128)(2,1)} %param.5), kind=kOutput, calls=%fused_computation.43 | convolution fusion | flops 4832624640 | bytes 14155776 | tf_op jit(solution)/shard_map/dot_general | solution.py:107
  101.6 2.9 collective-permute-start.14
  104.5 1.8 collective-permute-start.12
  107.8 2.1 collective-permute-done.14
  109.8 11.9 %collective-permute-done.13 = bf16[128,768]{1,0:T(8,128)(2,1)S(1)} collective-permute-done((bf16[128,768]{1,0:T(8,128)(2,1)S(1)}, bf16[128,768]{1,0:T(8,128)(2,1)S(1)}, u32[]{:S(2)}, u32[]{:S(2)}) %collective-permute-start.13) | collective-permute-done | bytes 196640 | tf_op jit(solution)/shard_map/ppermute | solution.py:40
  122.8 1.5 collective-permute-start.15
  124.3 19.3 %collective-permute-done.3 = bf16[512,1536]{1,0:T(8,128)(2,1)S(1)} collective-permute-done((bf16[512,1536]{1,0:T(8,128)(2,1)S(1)}, bf16[512,1536]{1,0:T(8,128)(2,1)S(1)}, u32[]{:S(2)}, u32[]{:S(2)}) %collective-permute-start.3) | collective-permute-done | bytes 1572896 | tf_op jit(solution)/shard_map/ppermute | solution.py:52
  144.6 9.5 %convolution_convert_fusion.5 = bf16[512,3072]{1,0:T(8,128)(2,1)S(1)} fusion(bf16[512,1536]{1,0:T(8,128)(2,1)S(1)} %multiply_convert_fusion.1, bf16[1536,3072]{1,0:T(8,128)(2,1)} %param.6), kind=kOutput, calls=%fused_computation.13 | convolution fusion | flops 4833411072 | bytes 14155776 | tf_op jit(solution)/shard_map/dot_general | solution.py:133
  154.1 1.6 dynamic-slice_bitcast_fusion.19
  157.0 10.3 %convolution_convert_fusion.7 = bf16[512,1536]{1,0:T(8,128)(2,1)} fusion(bf16[512,3072]{1,0:T(8,128)(2,1)} %all-gather.9.cloned.1.call-done, bf16[1536,3072]{1,0:T(8,128)(2,1)} %param.6), kind=kOutput, calls=%fused_computation.42 | convolution fusion | flops 4832624640 | bytes 14155776 | tf_op jit(solution)/shard_map/dot_general | solution.py:28
  167.3 9.6 %convolution_convert_fusion.6 = bf16[512,1536]{1,0:T(8,128)(2,1)S(1)} fusion(bf16[512,3072]{1,0:T(8,128)(2,1)} %all-gather.11.cloned.1.call-done, bf16[1536,3072]{1,0:T(8,128)(2,1)} %param.6), kind=kOutput, calls=%fused_computation.41 | convolution fusion | flops 4832624640 | bytes 14155776 | tf_op jit(solution)/shard_map/dot_general | solution.py:28
  177.1 2.3 multiply_convert_fusion
  179.4 9.7 %convolution_convert_fusion.4 = bf16[512,3072]{1,0:T(8,128)(2,1)S(1)} fusion(bf16[512,1536]{1,0:T(8,128)(2,1)S(1)} %multiply_convert_fusion, bf16[1536,3072]{1,0:T(8,128)(2,1)} %param.6), kind=kOutput, calls=%fused_computation.12 | convolution fusion | flops 4833411072 | bytes 14155776 | tf_op jit(solution)/shard_map/dot_general | solution.py:133
  189.2 1.5 collective-permute-start.18
  193.7 2.3 add_convert_fusion.3
  197.7 1.9 add_convert_fusion.2
  202.4 15.4 %collective-permute-done.5 = bf16[512,768]{1,0:T(8,128)(2,1)} collective-permute-done((bf16[512,768]{1,0:T(8,128)(2,1)}, bf16[512,768]{1,0:T(8,128)(2,1)}, u32[]{:S(2)}, u32[]{:S(2)}) %collective-permute-start.5) | collective-permute-done | bytes 786464 | tf_op jit(solution)/shard_map/ppermute | solution.py:84
  217.8 1.6 fusion.25
  219.3 14.7 %collective-permute-done.17 = bf16[512,768]{1,0:T(8,128)(2,1)} collective-permute-done((bf16[512,768]{1,0:T(8,128)(2,1)}, bf16[512,768]{1,0:T(8,128)(2,1)}, u32[]{:S(2)}, u32[]{:S(2)}) %collective-permute-start.17) | collective-permute-done | bytes 786464 | tf_op jit(solution)/shard_map/ppermute | solution.py:84
  234.0 1.7 fusion.24
  235.8 24.1 %collective-permute-done.18 = bf16[1024,1536]{1,0:T(8,128)(2,1)} collective-permute-done((bf16[1024,1536]{1,0:T(8,128)(2,1)S(1)}, bf16[1024,1536]{1,0:T(8,128)(2,1)}, u32[]{:S(2)}, u32[]{:S(2)}) %collective-permute-start.18) | collective-permute-done | bytes 3145760 | tf_op jit(solution)/shard_map/ppermute | solution.py:52
  259.8 5.7 %fusion.15 = (bf16[512,1536]{1,0:T(8,128)(2,1)S(1)}, bf16[512,1536]{1,0:T(8,128)(2,1)S(1)}) fusion(bf16[512,1536]{1,0:T(8,128)(2,1)S(1)} %copy-done.3, bf16[512,1536]{1,0:T(8,128)(2,1)S(1)} %copy-done.5, bf16[1024,1536]{1,0:T(8,128)(2,1)} %collective-permute-done.18, bf16[1024,1536]{1,0:T(8,128)(2,1)S(1)} %pad_maximum_fusion, ...), kind=kLoop, calls=%fused_computation.27 | loop fusion | flops 25165824 | bytes 15728640 | tf_op jit(solution)/shard_map/convert_element_type | solution.py:145
  265.6 5.3 %convolution_convert_fusion.2 = bf16[512,3072]{1,0:T(8,128)(2,1)S(1)} fusion(bf16[512,1536]{1,0:T(8,128)(2,1)S(1)} %get-tuple-element.42, bf16[3072,1536]{1,0:T(8,128)(2,1)S(1)} %bitcast.69), kind=kOutput, calls=%fused_computation.10 | convolution fusion | flops 4833411072 | bytes 14155776 | tf_op jit(solution)/shard_map/dot_general | solution.py:28
  270.9 9.1 %convolution_convert_fusion.3 = bf16[512,3072]{1,0:T(8,128)(2,1)S(1)} fusion(bf16[512,1536]{1,0:T(8,128)(2,1)S(1)} %get-tuple-element.40, bf16[3072,1536]{1,0:T(8,128)(2,1)} %param.5), kind=kOutput, calls=%fused_computation.11 | convolution fusion | flops 4833411072 | bytes 14155776 | tf_op jit(solution)/shard_map/dot_general | solution.py:28
  281.8 2.1 collective-permute-start.19
  285.0 3.0 collective-permute-start.22
  289.5 10.2 %collective-permute-start.24 = (bf16[128,768]{1,0:T(8,128)(2,1)S(1)}, bf16[128,768]{1,0:T(8,128)(2,1)S(1)}, u32[]{:S(2)}, u32[]{:S(2)}) collective-permute-start(bf16[128,768]{1,0:T(8,128)(2,1)S(1)} %get-tuple-element.70), channel_id=1, source_target_pairs={{0,8},{8,16},{16,24},{24,0},{1,9},{9,17},{17,25},{25,1},{2,10},{10... | collective-permute-start | bytes 589832 | tf_op jit(solution)/shard_map/ppermute | solution.py:93
  299.7 12.1 %collective-permute-done.20 = bf16[128,768]{1,0:T(8,128)(2,1)S(1)} collective-permute-done((bf16[128,768]{1,0:T(8,128)(2,1)S(1)}, bf16[128,768]{1,0:T(8,128)(2,1)S(1)}, u32[]{:S(2)}, u32[]{:S(2)}) %collective-permute-start.20) | collective-permute-done | bytes 196640 | tf_op jit(solution)/shard_map/ppermute | solution.py:93
  312.5 6.8 %collective-permute-done.23 = bf16[128,768]{1,0:T(8,128)(2,1)S(1)} collective-permute-done((bf16[128,768]{1,0:T(8,128)(2,1)S(1)}, bf16[128,768]{1,0:T(8,128)(2,1)S(1)}, u32[]{:S(2)}, u32[]{:S(2)}) %collective-permute-start.23) | collective-permute-done | bytes 196640 | tf_op jit(solution)/shard_map/ppermute | solution.py:93
  320.6 3.2 collective-permute-done.27
  324.0 5.6 %collective-permute-start.28 = (bf16[128,768]{1,0:T(8,128)(2,1)S(1)}, bf16[128,768]{1,0:T(8,128)(2,1)S(1)}, u32[]{:S(2)}, u32[]{:S(2)}) collective-permute-start(bf16[128,768]{1,0:T(8,128)(2,1)S(1)} %get-tuple-element.60), channel_id=1, source_target_pairs={{0,24},{8,0},{16,8},{24,16},{1,25},{9,1},{17,9},{25,17},{2,26},{10... | collective-permute-start | bytes 589832 | tf_op jit(solution)/shard_map/ppermute | solution.py:93
  331.0 12.4 %convolution_convert_fusion.1 = bf16[3072,1536]{1,0:T(8,128)(2,1)} fusion(bf16[512,3072]{1,0:T(8,128)(2,1)S(1)} %copy-done.15, bf16[512,3072]{1,0:T(8,128)(2,1)S(1)} %copy-done.14, bf16[512,1536]{1,0:T(8,128)(2,1)S(1)} %get-tuple-element.40, bf16[512,1536]{1,0:T(8,128)(2,1)S(1)} %get-tuple-element.42), kind=kOutput, calls=%fused_computation.1 | convolution fusion | flops 9687269376 | bytes 18874368 | tf_op jit(solution)/shard_map/dot_general | solution.py:22
  343.4 15.1 %convolution_convert_fusion = bf16[1536,3072]{1,0:T(8,128)(2,1)} fusion(bf16[512,3072]{1,0:T(8,128)(2,1)} %all-gather.11.cloned.1.call-done, bf16[512,3072]{1,0:T(8,128)(2,1)} %all-gather.9.cloned.1.call-done, bf16[512,1536]{1,0:T(8,128)(2,1)S(1)} %copy-done.11, bf16[512,1536]{1,0:T(8,128)(2,1)S(1)} %copy-done.9), kind=kOutput, calls=%fused_computation | convolution fusion | flops 9687269376 | bytes 18874368 | tf_op jit(solution)/shard_map/dot_general | solution.py:22
  358.7 3.2 collective-permute-start.32
  364.1 6.3 %collective-permute-done.32 = bf16[128,768]{1,0:T(8,128)(2,1)S(1)} collective-permute-done((bf16[128,768]{1,0:T(8,128)(2,1)S(1)}, bf16[128,768]{1,0:T(8,128)(2,1)S(1)}, u32[]{:S(2)}, u32[]{:S(2)}) %collective-permute-start.32) | collective-permute-done | bytes 196640 | tf_op jit(solution)/shard_map/ppermute | solution.py:93
  370.4 1.9 collective-permute-done.34
  372.3 6.6 %collective-permute-done.33 = bf16[128,768]{1,0:T(8,128)(2,1)S(1)} collective-permute-done((bf16[128,768]{1,0:T(8,128)(2,1)S(1)}, bf16[128,768]{1,0:T(8,128)(2,1)S(1)}, u32[]{:S(2)}, u32[]{:S(2)}) %collective-permute-start.33) | collective-permute-done | bytes 196640 | tf_op jit(solution)/shard_map/ppermute | solution.py:93
  (122 shorter events, 31.7 us)
Async XLA Ops:
  7.2 28.8 %copy-start.13 = (bf16[256,768]{1,0:T(8,128)(2,1)S(1)}, bf16[256,768]{1,0:T(8,128)(2,1)}, u32[]{:S(2)}) copy-start(bf16[256,768]{1,0:T(8,128)(2,1)} %param.7) | copy-start | bytes 1179652
  7.2 53.0 %all-gather.5.cloned.1.call-start = ((), (), s32[]{:S(2)}) async-start(), calls=%async_computation | async-start | bytes 3932160 | tf_op jit(solution)/shard_map/all_gather | solution.py:115
  8.3 10.5 %collective-permute-start.2 = (bf16[128,768]{1,0:T(8,128)(2,1)S(1)}, bf16[128,768]{1,0:T(8,128)(2,1)S(1)}, u32[]{:S(2)}, u32[]{:S(2)}) collective-permute-start(bf16[128,768]{1,0:T(8,128)(2,1)S(1)} %get-tuple-element.74), channel_id=1, source_target_pairs={{0,24},{8,0},{16,8},{24,16},{1,25},{9,1},{17,9},{25,17},{2,26},{10... | collective-permute-start | bytes 589832 | tf_op jit(solution)/shard_map/ppermute | solution.py:40
  13.4 16.7 %collective-permute-start.1 = (bf16[128,768]{1,0:T(8,128)(2,1)S(1)}, bf16[128,768]{1,0:T(8,128)(2,1)S(1)}, u32[]{:S(2)}, u32[]{:S(2)}) collective-permute-start(bf16[128,768]{1,0:T(8,128)(2,1)S(1)} %get-tuple-element.74), channel_id=1, source_target_pairs={{0,16},{8,24},{16,0},{24,8},{1,17},{9,25},{17,1},{25,9},{2,18},{10... | collective-permute-start | bytes 589832 | tf_op jit(solution)/shard_map/ppermute | solution.py:40
  13.4 16.7 %collective-permute-start = (bf16[128,768]{1,0:T(8,128)(2,1)S(1)}, bf16[128,768]{1,0:T(8,128)(2,1)S(1)}, u32[]{:S(2)}, u32[]{:S(2)}) collective-permute-start(bf16[128,768]{1,0:T(8,128)(2,1)S(1)} %get-tuple-element.74), channel_id=1, source_target_pairs={{0,8},{8,16},{16,24},{24,0},{1,9},{9,17},{17,25},{25,1},{2,10},{10... | collective-permute-start | bytes 589832 | tf_op jit(solution)/shard_map/ppermute | solution.py:40
  31.1 60.2 %all-gather.7.cloned.1.call-start = ((), (), s32[]{:S(2)}) async-start(), calls=%async_computation.1 | async-start | bytes 3932160 | tf_op jit(solution)/shard_map/all_gather | solution.py:115
  31.1 6.4 %collective-permute-start.8 = (bf16[128,768]{1,0:T(8,128)(2,1)S(1)}, bf16[128,768]{1,0:T(8,128)(2,1)S(1)}, u32[]{:S(2)}, u32[]{:S(2)}) collective-permute-start(bf16[128,768]{1,0:T(8,128)(2,1)S(1)} %get-tuple-element.24), channel_id=1, source_target_pairs={{0,24},{8,0},{16,8},{24,16},{1,25},{9,1},{17,9},{25,17},{2,26},{10... | collective-permute-start | bytes 589832 | tf_op jit(solution)/shard_map/ppermute | solution.py:40
  31.5 19.4 %collective-permute-start.7 = (bf16[128,768]{1,0:T(8,128)(2,1)S(1)}, bf16[128,768]{1,0:T(8,128)(2,1)S(1)}, u32[]{:S(2)}, u32[]{:S(2)}) collective-permute-start(bf16[128,768]{1,0:T(8,128)(2,1)S(1)} %get-tuple-element.24), channel_id=1, source_target_pairs={{0,16},{8,24},{16,0},{24,8},{1,17},{9,25},{17,1},{25,9},{2,18},{10... | collective-permute-start | bytes 589832 | tf_op jit(solution)/shard_map/ppermute | solution.py:40
  34.0 16.9 %collective-permute-start.6 = (bf16[128,768]{1,0:T(8,128)(2,1)S(1)}, bf16[128,768]{1,0:T(8,128)(2,1)S(1)}, u32[]{:S(2)}, u32[]{:S(2)}) collective-permute-start(bf16[128,768]{1,0:T(8,128)(2,1)S(1)} %get-tuple-element.24), channel_id=1, source_target_pairs={{0,8},{8,16},{16,24},{24,0},{1,9},{9,17},{17,25},{25,1},{2,10},{10... | collective-permute-start | bytes 589832 | tf_op jit(solution)/shard_map/ppermute | solution.py:40
  51.9 105.1 %all-gather.9.cloned.1.call-start = ((), (), s32[]{:S(2)}) async-start(), calls=%async_computation.2 | async-start | bytes 3932160 | tf_op jit(solution)/shard_map/all_gather | solution.py:115
  69.6 74.0 %copy-start.2 = (bf16[512,1536]{1,0:T(8,128)(2,1)}, bf16[512,1536]{1,0:T(8,128)(2,1)S(1)}, u32[]{:S(2)}) copy-start(bf16[512,1536]{1,0:T(8,128)(2,1)S(1)} %convolution_convert_fusion.9) | copy-start | bytes 4718596
  69.6 8.7 %collective-permute-start.11 = (bf16[128,768]{1,0:T(8,128)(2,1)S(1)}, bf16[128,768]{1,0:T(8,128)(2,1)S(1)}, u32[]{:S(2)}, u32[]{:S(2)}) collective-permute-start(bf16[128,768]{1,0:T(8,128)(2,1)S(1)} %get-tuple-element.27), channel_id=1, source_target_pairs={{0,24},{8,0},{16,8},{24,16},{1,25},{9,1},{17,9},{25,17},{2,26},{10... | collective-permute-start | bytes 589832 | tf_op jit(solution)/shard_map/ppermute | solution.py:40
  73.0 17.3 %collective-permute-start.10 = (bf16[128,768]{1,0:T(8,128)(2,1)S(1)}, bf16[128,768]{1,0:T(8,128)(2,1)S(1)}, u32[]{:S(2)}, u32[]{:S(2)}) collective-permute-start(bf16[128,768]{1,0:T(8,128)(2,1)S(1)} %get-tuple-element.27), channel_id=1, source_target_pairs={{0,16},{8,24},{16,0},{24,8},{1,17},{9,25},{17,1},{25,9},{2,18},{10... | collective-permute-start | bytes 589832 | tf_op jit(solution)/shard_map/ppermute | solution.py:40
  73.0 17.3 %collective-permute-start.9 = (bf16[128,768]{1,0:T(8,128)(2,1)S(1)}, bf16[128,768]{1,0:T(8,128)(2,1)S(1)}, u32[]{:S(2)}, u32[]{:S(2)}) collective-permute-start(bf16[128,768]{1,0:T(8,128)(2,1)S(1)} %get-tuple-element.27), channel_id=1, source_target_pairs={{0,8},{8,16},{16,24},{24,0},{1,9},{9,17},{17,25},{25,1},{2,10},{10... | collective-permute-start | bytes 589832 | tf_op jit(solution)/shard_map/ppermute | solution.py:40
  91.2 76.1 %all-gather.11.cloned.1.call-start = ((), (), s32[]{:S(2)}) async-start(), calls=%async_computation.3 | async-start | bytes 3932160 | tf_op jit(solution)/shard_map/all_gather | solution.py:120
  101.6 8.3 %collective-permute-start.14 = (bf16[128,768]{1,0:T(8,128)(2,1)S(1)}, bf16[128,768]{1,0:T(8,128)(2,1)S(1)}, u32[]{:S(2)}, u32[]{:S(2)}) collective-permute-start(bf16[128,768]{1,0:T(8,128)(2,1)S(1)} %get-tuple-element.30), channel_id=1, source_target_pairs={{0,24},{8,0},{16,8},{24,16},{1,25},{9,1},{17,9},{25,17},{2,26},{10... | collective-permute-start | bytes 589832 | tf_op jit(solution)/shard_map/ppermute | solution.py:40
  104.5 17.3 %collective-permute-start.13 = (bf16[128,768]{1,0:T(8,128)(2,1)S(1)}, bf16[128,768]{1,0:T(8,128)(2,1)S(1)}, u32[]{:S(2)}, u32[]{:S(2)}) collective-permute-start(bf16[128,768]{1,0:T(8,128)(2,1)S(1)} %get-tuple-element.30), channel_id=1, source_target_pairs={{0,16},{8,24},{16,0},{24,8},{1,17},{9,25},{17,1},{25,9},{2,18},{10... | collective-permute-start | bytes 589832 | tf_op jit(solution)/shard_map/ppermute | solution.py:40
  104.5 17.3 %collective-permute-start.12 = (bf16[128,768]{1,0:T(8,128)(2,1)S(1)}, bf16[128,768]{1,0:T(8,128)(2,1)S(1)}, u32[]{:S(2)}, u32[]{:S(2)}) collective-permute-start(bf16[128,768]{1,0:T(8,128)(2,1)S(1)} %get-tuple-element.30), channel_id=1, source_target_pairs={{0,8},{8,16},{16,24},{24,0},{1,9},{9,17},{17,25},{25,1},{2,10},{10... | collective-permute-start | bytes 589832 | tf_op jit(solution)/shard_map/ppermute | solution.py:40
  106.3 37.3 %collective-permute-start.3 = (bf16[512,1536]{1,0:T(8,128)(2,1)S(1)}, bf16[512,1536]{1,0:T(8,128)(2,1)S(1)}, u32[]{:S(2)}, u32[]{:S(2)}) collective-permute-start(bf16[512,1536]{1,0:T(8,128)(2,1)S(1)} %convolution_convert_fusion.9), channel_id=1, source_target_pairs={{0,4},{4,0},{1,5},{5,1},{2,6},{6,2},{3,7},{7,3},{8,12},{12,8},{9,1... | collective-permute-start | bytes 4718600 | tf_op jit(solution)/shard_map/ppermute | solution.py:52
  122.8 54.3 %collective-permute-start.15 = (bf16[512,1536]{1,0:T(8,128)(2,1)}, bf16[512,1536]{1,0:T(8,128)(2,1)}, u32[]{:S(2)}, u32[]{:S(2)}) collective-permute-start(bf16[512,1536]{1,0:T(8,128)(2,1)} %convolution_convert_fusion.8), channel_id=1, source_target_pairs={{0,4},{4,0},{1,5},{5,1},{2,6},{6,2},{3,7},{7,3},{8,12},{12,8},{9,1... | collective-permute-start | bytes 4718600 | tf_op jit(solution)/shard_map/ppermute | solution.py:52
  157.0 36.7 %collective-permute-start.4 = (bf16[2,512,768]{2,1,0:T(8,128)(2,1)}, bf16[2,512,768]{2,1,0:T(8,128)(2,1)}, u32[]{:S(2)}, u32[]{:S(2)}) collective-permute-start(bf16[2,512,768]{2,1,0:T(8,128)(2,1)} %pad_maximum_fusion.1), channel_id=1, source_target_pairs={{0,1},{1,0},{2,3},{3,2},{4,5},{5,4},{6,7},{7,6},{8,9},{9,8},{10,11... | collective-permute-start | bytes 4718600 | tf_op jit(solution)/shard_map/ppermute | solution.py:74
  189.2 70.7 %collective-permute-start.18 = (bf16[1024,1536]{1,0:T(8,128)(2,1)S(1)}, bf16[1024,1536]{1,0:T(8,128)(2,1)}, u32[]{:S(2)}, u32[]{:S(2)}) collective-permute-start(bf16[1024,1536]{1,0:T(8,128)(2,1)S(1)} %pad_maximum_fusion), channel_id=1, source_target_pairs={{0,4},{4,0},{1,5},{5,1},{2,6},{6,2},{3,7},{7,3},{8,12},{12,8},{9,1... | collective-permute-start | bytes 9437192 | tf_op jit(solution)/shard_map/ppermute | solution.py:52
  193.5 4.2 %collective-permute-start.16 = (bf16[2,512,768]{2,1,0:T(8,128)(2,1)}, bf16[2,512,768]{2,1,0:T(8,128)(2,1)}, u32[]{:S(2)}, u32[]{:S(2)}) collective-permute-start(bf16[2,512,768]{2,1,0:T(8,128)(2,1)} %pad_maximum_fusion.2), channel_id=1, source_target_pairs={{0,1},{1,0},{2,3},{3,2},{4,5},{5,4},{6,7},{7,6},{8,9},{9,8},{10,11... | collective-permute-start | bytes 4718600 | tf_op jit(solution)/shard_map/ppermute | solution.py:74
  197.1 20.7 %collective-permute-start.5 = (bf16[512,768]{1,0:T(8,128)(2,1)}, bf16[512,768]{1,0:T(8,128)(2,1)}, u32[]{:S(2)}, u32[]{:S(2)}) collective-permute-start(bf16[512,768]{1,0:T(8,128)(2,1)} %dynamic-slice_bitcast_fusion.15), channel_id=1, source_target_pairs={{0,2},{1,3},{2,0},{3,1},{4,6},{5,7},{6,4},{7,5},{8,10},{9,11},{10,... | collective-permute-start | bytes 2359304 | tf_op jit(solution)/shard_map/ppermute | solution.py:84
  201.0 33.1 %collective-permute-start.17 = (bf16[512,768]{1,0:T(8,128)(2,1)}, bf16[512,768]{1,0:T(8,128)(2,1)}, u32[]{:S(2)}, u32[]{:S(2)}) collective-permute-start(bf16[512,768]{1,0:T(8,128)(2,1)} %dynamic-slice_bitcast_fusion.10), channel_id=1, source_target_pairs={{0,2},{1,3},{2,0},{3,1},{4,6},{5,7},{6,4},{7,5},{8,10},{9,11},{10,... | collective-permute-start | bytes 2359304 | tf_op jit(solution)/shard_map/ppermute | solution.py:84
  202.4 57.4 %copy-start.3 = (bf16[512,1536]{1,0:T(8,128)(2,1)S(1)}, bf16[512,1536]{1,0:T(8,128)(2,1)}, u32[]{:S(2)}) copy-start(bf16[512,1536]{1,0:T(8,128)(2,1)} %copy-done.2) | copy-start | bytes 4718596
  202.4 57.4 %copy-start.5 = (bf16[512,1536]{1,0:T(8,128)(2,1)S(1)}, bf16[512,1536]{1,0:T(8,128)(2,1)}, u32[]{:S(2)}) copy-start(bf16[512,1536]{1,0:T(8,128)(2,1)} %copy-done.4) | copy-start | bytes 4718596
  234.0 31.5 %slice-start = ((s8[9437184]{0:T(1024)(128)(4,1)}), s8[4194304]{0:T(1024)(128)(4,1)S(1)}, s32[]{:S(2)}) async-start(s8[9437184]{0:T(1024)(128)(4,1)} %bitcast.68), calls=%async_computation.4 | async-start | bytes 8388608
  235.7 29.8 %slice-start.1 = ((s8[9437184]{0:T(1024)(128)(4,1)}), s8[4194304]{0:T(1024)(128)(4,1)S(1)}, s32[]{:S(2)}) async-start(s8[9437184]{0:T(1024)(128)(4,1)} %bitcast.68), calls=%async_computation.5 | async-start | bytes 8388608
  235.7 29.8 %slice-start.2 = ((s8[9437184]{0:T(1024)(128)(4,1)}), s8[1048576]{0:T(1024)(128)(4,1)S(1)}, s32[]{:S(2)}) async-start(s8[9437184]{0:T(1024)(128)(4,1)} %bitcast.68), calls=%async_computation.6 | async-start | bytes 2097152
  281.0 4.1 %collective-permute-start.26 = (bf16[2,512,768]{2,1,0:T(8,128)(2,1)S(1)}, bf16[2,512,768]{2,1,0:T(8,128)(2,1)S(1)}, u32[]{:S(2)}, u32[]{:S(2)}) collective-permute-start(bf16[2,512,768]{2,1,0:T(8,128)(2,1)S(1)} %pad_maximum_fusion.4), channel_id=1, source_target_pairs={{0,1},{1,0},{2,3},{3,2},{4,5},{5,4},{6,7},{7,6},{8,9},{9,8},{10,11... | collective-permute-start | bytes 4718600 | tf_op jit(solution)/shard_map/ppermute | solution.py:74
  281.2 39.0 %collective-permute-start.25 = (bf16[2,512,768]{2,1,0:T(8,128)(2,1)S(1)}, bf16[2,512,768]{2,1,0:T(8,128)(2,1)S(1)}, u32[]{:S(2)}, u32[]{:S(2)}) collective-permute-start(bf16[2,512,768]{2,1,0:T(8,128)(2,1)S(1)} %pad_maximum_fusion.3), channel_id=1, source_target_pairs={{0,1},{1,0},{2,3},{3,2},{4,5},{5,4},{6,7},{7,6},{8,9},{9,8},{10,11... | collective-permute-start | bytes 4718600 | tf_op jit(solution)/shard_map/ppermute | solution.py:74
  281.8 7.7 %collective-permute-start.19 = (bf16[128,768]{1,0:T(8,128)(2,1)S(1)}, bf16[128,768]{1,0:T(8,128)(2,1)S(1)}, u32[]{:S(2)}, u32[]{:S(2)}) collective-permute-start(bf16[128,768]{1,0:T(8,128)(2,1)S(1)} %get-tuple-element.66), channel_id=1, source_target_pairs={{0,24},{8,0},{16,8},{24,16},{1,25},{9,1},{17,9},{25,17},{2,26},{10... | collective-permute-start | bytes 589832 | tf_op jit(solution)/shard_map/ppermute | solution.py:93
  283.8 15.9 %collective-permute-start.21 = (bf16[128,768]{1,0:T(8,128)(2,1)S(1)}, bf16[128,768]{1,0:T(8,128)(2,1)S(1)}, u32[]{:S(2)}, u32[]{:S(2)}) collective-permute-start(bf16[128,768]{1,0:T(8,128)(2,1)S(1)} %get-tuple-element.67), channel_id=1, source_target_pairs={{0,8},{8,16},{16,24},{24,0},{1,9},{9,17},{17,25},{25,1},{2,10},{10... | collective-permute-start | bytes 589832 | tf_op jit(solution)/shard_map/ppermute | solution.py:93
  283.9 27.9 %collective-permute-start.20 = (bf16[128,768]{1,0:T(8,128)(2,1)S(1)}, bf16[128,768]{1,0:T(8,128)(2,1)S(1)}, u32[]{:S(2)}, u32[]{:S(2)}) collective-permute-start(bf16[128,768]{1,0:T(8,128)(2,1)S(1)} %get-tuple-element.68), channel_id=1, source_target_pairs={{0,16},{8,24},{16,0},{24,8},{1,17},{9,25},{17,1},{25,9},{2,18},{10... | collective-permute-start | bytes 589832 | tf_op jit(solution)/shard_map/ppermute | solution.py:93
  285.0 27.4 %collective-permute-start.22 = (bf16[128,768]{1,0:T(8,128)(2,1)S(1)}, bf16[128,768]{1,0:T(8,128)(2,1)S(1)}, u32[]{:S(2)}, u32[]{:S(2)}) collective-permute-start(bf16[128,768]{1,0:T(8,128)(2,1)S(1)} %get-tuple-element.69), channel_id=1, source_target_pairs={{0,24},{8,0},{16,8},{24,16},{1,25},{9,1},{17,9},{25,17},{2,26},{10... | collective-permute-start | bytes 589832 | tf_op jit(solution)/shard_map/ppermute | solution.py:93
  289.5 23.0 %collective-permute-start.24 = (bf16[128,768]{1,0:T(8,128)(2,1)S(1)}, bf16[128,768]{1,0:T(8,128)(2,1)S(1)}, u32[]{:S(2)}, u32[]{:S(2)}) collective-permute-start(bf16[128,768]{1,0:T(8,128)(2,1)S(1)} %get-tuple-element.70), channel_id=1, source_target_pairs={{0,8},{8,16},{16,24},{24,0},{1,9},{9,17},{17,25},{25,1},{2,10},{10... | collective-permute-start | bytes 589832 | tf_op jit(solution)/shard_map/ppermute | solution.py:93
  299.7 19.6 %collective-permute-start.23 = (bf16[128,768]{1,0:T(8,128)(2,1)S(1)}, bf16[128,768]{1,0:T(8,128)(2,1)S(1)}, u32[]{:S(2)}, u32[]{:S(2)}) collective-permute-start(bf16[128,768]{1,0:T(8,128)(2,1)S(1)} %get-tuple-element.71), channel_id=1, source_target_pairs={{0,16},{8,24},{16,0},{24,8},{1,17},{9,25},{17,1},{25,9},{2,18},{10... | collective-permute-start | bytes 589832 | tf_op jit(solution)/shard_map/ppermute | solution.py:93
  311.8 12.0 %collective-permute-start.27 = (bf16[512,768]{1,0:T(8,128)(2,1)S(1)}, bf16[512,768]{1,0:T(8,128)(2,1)S(1)}, u32[]{:S(2)}, u32[]{:S(2)}) collective-permute-start(bf16[512,768]{1,0:T(8,128)(2,1)S(1)} %dynamic-slice_bitcast_fusion.1), channel_id=1, source_target_pairs={{0,2},{1,3},{2,0},{3,1},{4,6},{5,7},{6,4},{7,5},{8,10},{9,11},{10,... | collective-permute-start | bytes 2359304 | tf_op jit(solution)/shard_map/ppermute | solution.py:84
  324.0 38.6 %collective-permute-start.28 = (bf16[128,768]{1,0:T(8,128)(2,1)S(1)}, bf16[128,768]{1,0:T(8,128)(2,1)S(1)}, u32[]{:S(2)}, u32[]{:S(2)}) collective-permute-start(bf16[128,768]{1,0:T(8,128)(2,1)S(1)} %get-tuple-element.60), channel_id=1, source_target_pairs={{0,24},{8,0},{16,8},{24,16},{1,25},{9,1},{17,9},{25,17},{2,26},{10... | collective-permute-start | bytes 589832 | tf_op jit(solution)/shard_map/ppermute | solution.py:93
  329.7 34.3 %collective-permute-start.30 = (bf16[128,768]{1,0:T(8,128)(2,1)S(1)}, bf16[128,768]{1,0:T(8,128)(2,1)S(1)}, u32[]{:S(2)}, u32[]{:S(2)}) collective-permute-start(bf16[128,768]{1,0:T(8,128)(2,1)S(1)} %get-tuple-element.61), channel_id=1, source_target_pairs={{0,8},{8,16},{16,24},{24,0},{1,9},{9,17},{17,25},{25,1},{2,10},{10... | collective-permute-start | bytes 589832 | tf_op jit(solution)/shard_map/ppermute | solution.py:93
  329.7 34.3 %collective-permute-start.29 = (bf16[128,768]{1,0:T(8,128)(2,1)S(1)}, bf16[128,768]{1,0:T(8,128)(2,1)S(1)}, u32[]{:S(2)}, u32[]{:S(2)}) collective-permute-start(bf16[128,768]{1,0:T(8,128)(2,1)S(1)} %get-tuple-element.62), channel_id=1, source_target_pairs={{0,16},{8,24},{16,0},{24,8},{1,17},{9,25},{17,1},{25,9},{2,18},{10... | collective-permute-start | bytes 589832 | tf_op jit(solution)/shard_map/ppermute | solution.py:93
  330.4 13.0 %copy-start.9 = (bf16[512,1536]{1,0:T(8,128)(2,1)S(1)}, bf16[512,1536]{1,0:T(8,128)(2,1)}, u32[]{:S(2)}) copy-start(bf16[512,1536]{1,0:T(8,128)(2,1)} %copy-done.8) | copy-start | bytes 4718596
  330.4 13.0 %copy-start.11 = (bf16[512,1536]{1,0:T(8,128)(2,1)S(1)}, bf16[512,1536]{1,0:T(8,128)(2,1)}, u32[]{:S(2)}) copy-start(bf16[512,1536]{1,0:T(8,128)(2,1)} %copy-done.10) | copy-start | bytes 4718596
  330.4 28.1 %collective-permute-start.31 = (bf16[512,768]{1,0:T(8,128)(2,1)S(1)}, bf16[512,768]{1,0:T(8,128)(2,1)S(1)}, u32[]{:S(2)}, u32[]{:S(2)}) collective-permute-start(bf16[512,768]{1,0:T(8,128)(2,1)S(1)} %dynamic-slice_bitcast_fusion), channel_id=1, source_target_pairs={{0,2},{1,3},{2,0},{3,1},{4,6},{5,7},{6,4},{7,5},{8,10},{9,11},{10,... | collective-permute-start | bytes 2359304 | tf_op jit(solution)/shard_map/ppermute | solution.py:84
  358.7 11.7 %collective-permute-start.32 = (bf16[128,768]{1,0:T(8,128)(2,1)S(1)}, bf16[128,768]{1,0:T(8,128)(2,1)S(1)}, u32[]{:S(2)}, u32[]{:S(2)}) collective-permute-start(bf16[128,768]{1,0:T(8,128)(2,1)S(1)} %get-tuple-element.63), channel_id=1, source_target_pairs={{0,24},{8,0},{16,8},{24,16},{1,25},{9,1},{17,9},{25,17},{2,26},{10... | collective-permute-start | bytes 589832 | tf_op jit(solution)/shard_map/ppermute | solution.py:93
  362.0 10.4 %collective-permute-start.34 = (bf16[128,768]{1,0:T(8,128)(2,1)S(1)}, bf16[128,768]{1,0:T(8,128)(2,1)S(1)}, u32[]{:S(2)}, u32[]{:S(2)}) collective-permute-start(bf16[128,768]{1,0:T(8,128)(2,1)S(1)} %get-tuple-element.64), channel_id=1, source_target_pairs={{0,8},{8,16},{16,24},{24,0},{1,9},{9,17},{17,25},{25,1},{2,10},{10... | collective-permute-start | bytes 589832 | tf_op jit(solution)/shard_map/ppermute | solution.py:93
  362.6 16.4 %collective-permute-start.33 = (bf16[128,768]{1,0:T(8,128)(2,1)S(1)}, bf16[128,768]{1,0:T(8,128)(2,1)S(1)}, u32[]{:S(2)}, u32[]{:S(2)}) collective-permute-start(bf16[128,768]{1,0:T(8,128)(2,1)S(1)} %get-tuple-element.65), channel_id=1, source_target_pairs={{0,16},{8,24},{16,0},{24,8},{1,17},{9,25},{17,1},{25,9},{2,18},{10... | collective-permute-start | bytes 589832 | tf_op jit(solution)/shard_map/ppermute | solution.py:93
  (10 other events, 73.4 us)
Sparse Core Ops, SparseCore 0:
  31.2 28.9 all-gather.4
  62.3 28.5 all-gather.6
  93.0 28.5 all-gather.8
  123.0 28.5 all-gather.10
